TPU v7x, 256 devices: a whole 4x4x8 slice. The times are simulated.
256 devices in a mesh: outer: 16 (over y_hi, x, core), inner: 16 (over y_lo, z).
Axes of the slice: x: 4, y: 4 (y_hi: 2, y_lo: 2; y = y_hi * 2 + y_lo), z: 8, core: 2. Of those that a mesh axis runs over, the one named last changes fastest.
Arguments:
- images: bfloat16 [32768, 384], P(('outer', 'inner')), may hold values from -4 to 4
- texts: bfloat16 [32768, 384], P(('outer', 'inner')), may hold values from -4 to 4
- logit_scale: float32 [1], replicated, may hold values from 8 to 16
Outputs:
- loss: float32 [1], replicated
- grad_image: float32 [32768, 384], P(('outer', 'inner'))
- grad_text: float32 [32768, 384], P(('outer', 'inner'))
All inputs are finite; a program needn't handle non-finite values.
Results may differ from a plain program's by a relative error of at most 0.0018.
Values may be sent and summed in bfloat16 or wider, within the bound.
A program may use at most 64 MiB of HBM per device.

v0:
```python
import jax
import jax.numpy as jnp
from jax import lax
from jax.sharding import PartitionSpec as P


def merged(value, axis, join):
    pieces = jax.tree.map(lambda part: lax.all_gather(part, axis), value)
    head = jax.tree.map(lambda part: part[0], pieces)
    tail = jax.tree.map(lambda part: part[1:], pieces)
    total, _ = lax.scan(lambda total, share: (join(total, share), None), head, tail)
    return total


def block_split(image_rows):
    total_rows, width = image_rows.shape
    block_rows = min(total_rows, 256)
    return image_rows.reshape(total_rows // block_rows, block_rows, width)


def first_pass(image_rows, text_rows, factor):
    image_blocks = block_split(image_rows)
    column_count = text_rows.shape[0]

    def first_advance(carry, block):
        column_max, column_sum = carry
        score_tile = factor * jnp.einsum(
            "re,ce->rc", block, text_rows, preferred_element_type=jnp.float32
        )
        row_max = score_tile.max(1)
        row_sum = jnp.sum(jnp.exp(score_tile - row_max[:, None]), 1)
        new_max = jnp.maximum(column_max, score_tile.max(0))
        column_sum = column_sum * jnp.exp(column_max - new_max) + jnp.sum(
            jnp.exp(score_tile - new_max[None, :]), 0
        )
        return ((new_max, column_sum), (row_max, row_sum))

    initial = (
        jnp.full((column_count,), -1e30, jnp.float32),
        jnp.zeros((column_count,), jnp.float32),
    )
    (column_max, column_sum), (row_max, row_sum) = lax.scan(first_advance, initial, image_blocks)
    return ((row_max.reshape(-1), row_sum.reshape(-1)), (column_max, column_sum))


def second_pass(image_rows, text_rows, lse_image, lse_text, factor):
    image_blocks = block_split(image_rows)
    lse_blocks = lse_image.reshape(image_blocks.shape[0], image_blocks.shape[1])

    def second_advance(text_total, inputs):
        block, block_lse = inputs
        score_tile = factor * jnp.einsum(
            "re,ce->rc", block, text_rows, preferred_element_type=jnp.float32
        )
        weights = (
            (jnp.exp(score_tile - block_lse[:, None]) + jnp.exp(score_tile - lse_text[None, :]))
            * 0.5
        ).astype(jnp.bfloat16)
        image_part = jnp.dot(weights, text_rows, preferred_element_type=jnp.float32)
        text_total = text_total + jnp.einsum(
            "rc,re->ce", weights, block, preferred_element_type=jnp.float32
        )
        return (text_total, image_part)

    initial = jnp.zeros(text_rows.shape, jnp.float32)
    text_total, image_parts = lax.scan(second_advance, initial, (image_blocks, lse_blocks))
    return (image_parts.reshape(image_rows.shape), text_total)


def combine_parts(first, second):
    top_value = jnp.maximum(first[0], second[0])
    return (
        top_value,
        first[1] * jnp.exp(first[0] - top_value) + second[1] * jnp.exp(second[0] - top_value),
    )


def local(images, texts, logit_scale):
    factor = logit_scale[0]
    row_count = images.shape[0]
    diagonal = factor * jnp.sum(images.astype(jnp.float32) * texts.astype(jnp.float32), 1)
    image_rows = lax.all_gather(images, "inner", axis=0, tiled=True)
    text_rows = lax.all_gather(texts, "outer", axis=0, tiled=True)
    row_parts, column_parts = first_pass(image_rows, text_rows, factor)
    row_max, row_sum = merged(row_parts, "inner", combine_parts)
    column_max, column_sum = merged(column_parts, "outer", combine_parts)
    lse_image = row_max + jnp.log(row_sum)
    lse_text = column_max + jnp.log(column_sum)
    image_parts, text_parts = second_pass(image_rows, text_rows, lse_image, lse_text, factor)
    image_total = lax.psum_scatter(image_parts, "inner", scatter_dimension=0, tiled=True)
    text_total = lax.psum_scatter(text_parts, "outer", scatter_dimension=0, tiled=True)
    image_start = lax.axis_index("inner") * row_count
    text_start = lax.axis_index("outer") * row_count
    lse_row = lax.dynamic_slice_in_dim(lse_image, image_start, row_count)
    lse_col = lax.dynamic_slice_in_dim(lse_text, text_start, row_count)
    local_terms = jnp.sum(lse_row) + jnp.sum(lse_col) - 2.0 * jnp.sum(diagonal)
    total_terms = lax.psum(local_terms, ("outer", "inner"))
    total_pairs = row_count * lax.axis_size("outer") * lax.axis_size("inner")
    loss = (total_terms / (2.0 * total_pairs)).reshape(1)
    grad_image = factor * (image_total - texts.astype(jnp.float32))
    grad_text = factor * (text_total - images.astype(jnp.float32))
    return (loss, grad_image, grad_text)


def solution(mesh):
    in_specs = (P(("outer", "inner"), None), P(("outer", "inner"), None), P())
    out_specs = (P(), P(("outer", "inner"), None), P(("outer", "inner"), None))
    return jax.shard_map(local, mesh=mesh, in_specs=in_specs, out_specs=out_specs, check_vma=False)
```

profile of v0, /device:TPU:1, one launch (start us, length us, event | category | flops | bytes accessed | tf_op | source)
XLA Modules:
  0.0 584.3 jit_solution(10611504395151975999)
XLA Ops:
  7.2 0.0 all-gather.7.cloned.1.call-start
  7.2 0.7 all-gather.7.cloned.1.call-update
  7.9 0.0 all-gather.9.cloned.1.call-start
  7.9 0.7 all-gather.9.cloned.1.call-update
  8.6 0.0 reduce-scatter.5.cloned.1.call-start
  8.8 65.7 %all-gather.7.cloned.1.call-done = bf16[2048,384]{1,0:T(8,128)(2,1)} async-done(((bf16[128,384]{1,0:T(8,128)(2,1)}), bf16[2048,384]{1,0:T(8,128)(2,1)}) %all-gather.7.cloned.1.call-update) | async-done | bytes 1572880 | tf_op jit(solution)/shard_map/all_gather | solution.py:82
  74.5 61.7 %all-gather.9.cloned.1.call-done = bf16[2048,384]{1,0:T(8,128)(2,1)} async-done(((bf16[128,384]{1,0:T(8,128)(2,1)}), bf16[2048,384]{1,0:T(8,128)(2,1)}) %all-gather.9.cloned.1.call-update) | async-done | bytes 1572880 | tf_op jit(solution)/shard_map/all_gather | solution.py:83
  136.2 30.9 %while.56 = (s32[]{:T(128)}, f32[2048]{0:T(1024)S(1)}, f32[2048]{0:T(1024)S(1)}, f32[8,256]{1,0:T(8,128)S(1)}, f32[8,256]{1,0:T(8,128)S(1)}, /*index=5*/f32[]{:T...) while((s32[]{:T(128)}, f32[2048]{0:T(1024)S(1)}, ...), condition=%wide.region_5.0_spmd.clone, body=%wide.region_0.5_spmd.clone.sunk | while | flops 406332928 | bytes 6078084 | solution.py:42
  136.2 3.0 fusion.31
  139.2 0.7 exponential_reduce_fusion.3
  140.1 3.0 fusion.31
  143.1 0.7 exponential_reduce_fusion.3
  143.9 3.0 fusion.31
  146.9 0.7 exponential_reduce_fusion.3
  147.8 3.0 fusion.31
  150.8 0.7 exponential_reduce_fusion.3
  151.7 3.0 fusion.31
  154.7 0.7 exponential_reduce_fusion.3
  155.5 3.0 fusion.31
  158.5 0.7 exponential_reduce_fusion.3
  159.4 3.0 fusion.31
  162.4 0.7 exponential_reduce_fusion.3
  163.2 3.0 fusion.31
  166.3 0.7 exponential_reduce_fusion.3
  167.1 21.8 %all-gather = f32[32768]{0:T(1024)S(1)} all-gather(f32[2048]{0:T(1024)S(1)} %get-tuple-element.151), channel_id=2, replica_groups=mesh['outer'=16,'inner'=16] {'outer'}, dimensions={0}, use_global_device_ids=true | all-gather | bytes 139264 | tf_op jit(solution)/shard_map/all_gather | solution.py:8
  189.0 19.6 %all-gather.1 = f32[32768]{0:T(1024)S(1)} all-gather(f32[2048]{0:T(1024)S(1)} %get-tuple-element.152), channel_id=3, replica_groups=mesh['outer'=16,'inner'=16] {'outer'}, dimensions={0}, use_global_device_ids=true | all-gather | bytes 139264 | tf_op jit(solution)/shard_map/all_gather | solution.py:8
  208.6 27.2 %all-gather.2 = f32[16,1,2048]{2,1,0:T(1,128)S(1)} all-gather(f32[1,1,2048]{2,1,0:T(1,128)S(1)} %reshape.36), channel_id=1, replica_groups=mesh['outer'=16,'inner'=16] {'inner'}, dimensions={0}, use_global_device_ids=true | all-gather | bytes 139264 | tf_op jit(solution)/shard_map/all_gather | solution.py:8
  235.8 23.2 %all-gather.3 = f32[16,1,2048]{2,1,0:T(1,128)S(1)} all-gather(f32[1,1,2048]{2,1,0:T(1,128)S(1)} %reshape.38), channel_id=1, replica_groups=mesh['outer'=16,'inner'=16] {'inner'}, dimensions={0}, use_global_device_ids=true | all-gather | bytes 139264 | tf_op jit(solution)/shard_map/all_gather | solution.py:8
  259.2 0.9 while.55
  260.2 0.9 while.54
  261.2 66.6 %while.57 = (s32[]{:T(128)}, f32[2048,384]{1,0:T(8,128)}, f32[8,256,384]{2,1,0:T(8,128)}, f32[]{:T(128)}, bf16[8,256,384]{2,1,0:T(8,128)(2,1)}, /*index=5*/bf16[...) while((s32[]{:T(128)}, f32[2048,384]{1,0:T(8,128)}, ...), condition=%wide.region_16.17_spmd.clone, body=%wide.region_15.16_spmd.clone.sunk | while | flops 1212678144 | bytes 13381255 | solution.py:66
  261.2 2.6 multiply_convert_fusion.2
  263.8 3.3 select_add_fusion.2
  267.2 1.5 fusion.39
  268.6 2.6 multiply_convert_fusion.2
  271.2 4.4 select_add_fusion.2
  275.6 1.4 fusion.39
  277.1 2.6 multiply_convert_fusion.2
  279.6 4.4 select_add_fusion.2
  284.1 1.4 fusion.39
  285.5 2.6 multiply_convert_fusion.2
  288.1 4.4 select_add_fusion.2
  292.5 1.5 fusion.39
  294.0 2.6 multiply_convert_fusion.2
  296.5 4.4 select_add_fusion.2
  301.0 1.5 fusion.39
  302.4 2.6 multiply_convert_fusion.2
  305.0 4.4 select_add_fusion.2
  309.4 1.5 fusion.39
  310.9 2.6 multiply_convert_fusion.2
  313.5 4.4 select_add_fusion.2
  317.9 1.5 fusion.39
  319.4 2.6 multiply_convert_fusion.2
  321.9 4.4 select_add_fusion.2
  326.4 1.5 fusion.39
  327.8 0.0 reduce-scatter.5.cloned.1.call-update
  327.9 0.0 reduce-scatter.3.cloned.1.call-start
  327.9 0.5 reduce-scatter.3.cloned.1.call-update
  329.1 0.7 dynamic-slice_reduce_fusion
  331.1 88.4 %reduce-scatter.5.cloned.1.call-done = f32[128,384]{1,0:T(8,128)} async-done(((f32[2048,384]{1,0:T(8,128)}), f32[128,384]{1,0:T(8,128)}) %reduce-scatter.5.cloned.1.call-update) | async-done | bytes 196624 | tf_op jit(solution)/shard_map/reduce_scatter | solution.py:91
  419.5 70.1 %reduce-scatter.3.cloned.1.call-done = f32[128,384]{1,0:T(8,128)} async-done(((f32[2048,384]{1,0:T(8,128)}), f32[128,384]{1,0:T(8,128)}) %reduce-scatter.3.cloned.1.call-update) | async-done | bytes 196624 | tf_op jit(solution)/shard_map/reduce_scatter | solution.py:90
  489.6 1.8 fusion.11
  491.4 0.6 multiply_reduce_fusion
  492.7 83.3 %psum.7 = f32[]{:T(128)} all-reduce(f32[]{:T(128)S(6)} %sub.58), channel_id=1, replica_groups=mesh['outer'=16,'inner'=16] {'outer','inner'}, use_global_device_ids=true, to_apply=%region_14.15 | all-reduce | flops 1 | bytes 8 | tf_op jit(solution)/shard_map/psum | solution.py:97
  (137 shorter events, 2.1 us)
Async XLA Ops:
  7.2 67.3 %all-gather.7.cloned.1.call-start = ((), (), s32[]{:S(2)}) async-start(), calls=%async_computation.2 | async-start | bytes 1671168 | tf_op jit(solution)/shard_map/all_gather | solution.py:82
  7.9 128.3 %all-gather.9.cloned.1.call-start = ((), (), s32[]{:S(2)}) async-start(), calls=%async_computation.3 | async-start | bytes 1671168 | tf_op jit(solution)/shard_map/all_gather | solution.py:83
  8.6 410.8 %reduce-scatter.5.cloned.1.call-start = ((), (), s32[]{:S(2)}) async-start(), calls=%async_computation.5 | async-start | bytes 3342336 | tf_op jit(solution)/shard_map/reduce_scatter | solution.py:91
  167.1 94.1 %copy-start = (bf16[2048,384]{1,0:T(8,128)(2,1)S(1)}, bf16[2048,384]{1,0:T(8,128)(2,1)}, u32[]{:S(2)}) copy-start(bf16[2048,384]{1,0:T(8,128)(2,1)} %get-tuple-element.568) | copy-start | bytes 4718596
  327.9 161.7 %copy-start.1 = (bf16[128,384]{1,0:T(8,128)(2,1)S(1)}, bf16[128,384]{1,0:T(8,128)(2,1)}, u32[]{:S(2)}) copy-start(bf16[128,384]{1,0:T(8,128)(2,1)} %param.11) | copy-start | bytes 294916
  327.9 161.7 %copy-start.2 = (bf16[128,384]{1,0:T(8,128)(2,1)S(1)}, bf16[128,384]{1,0:T(8,128)(2,1)}, u32[]{:S(2)}) copy-start(bf16[128,384]{1,0:T(8,128)(2,1)} %param.12) | copy-start | bytes 294916
  327.9 161.7 %reduce-scatter.3.cloned.1.call-start = ((), (), s32[]{:S(2)}) async-start(), calls=%async_computation.4 | async-start | bytes 3342336 | tf_op jit(solution)/shard_map/reduce_scatter | solution.py:90
Sparse Core Ops, SparseCore 0:
  9.8 64.6 all-gather.6
  77.2 58.9 all-gather.8
  328.0 91.4 reduce-scatter.4
  421.9 67.6 reduce-scatter.2
where the time goes:
time: 585 us; the launch traced here: 584 us
  waiting for transfers between devices  288 us (49%)
  blocking collectives  175 us (30%)
  matrix products  90.5 us (15%)
  between operations  18.3 us (3%)
  other arithmetic  9.33 us (2%)
    all_gather x4, blocking collectives, merged(): pieces = jax.tree.map(lambda part: lax.all_gather(part, axis), value)  91.9 us
    reduce_scatter x1, waiting for transfers between devices, local(): lax.psum_scatter(text_parts, 'outer', scatter_dimension=0, tiled=True)  88.4 us
    psum x1, blocking collectives, local(): total_terms = lax.psum(local_terms, ('outer', 'inner'))  83.3 us
    reduce_scatter x1, waiting for transfers between devices, local(): lax.psum_scatter(image_parts, 'inner', scatter_dimension=0, tiled=True)  70.1 us
    all_gather x1, waiting for transfers between devices, local(): image_rows = lax.all_gather(images, 'inner', axis=0, tiled=True)  65.7 us
    all_gather x1, waiting for transfers between devices, local(): text_rows = lax.all_gather(texts, 'outer', axis=0, tiled=True)  61.7 us
    dot_general x8, matrix products, second_advance(): jnp.einsum('rc,re->ce', weights, block, preferred_element_type=jnp.float32)  34.3 us
    dot_general x8, matrix products, first_advance(): jnp.einsum('re,ce->rc', block, text_rows, preferred_element_type=jnp.floa...  24 us
  transfers between devices with their start and end apart: 4, of which 4 were waited for; matrix products, arithmetic and copies ran while one was open for 0% of the time, Pallas kernels for 0%

commit v1 on v0

v1 whole, which is shorter than its diff:
```python
import math

import jax
import jax.numpy as jnp
from jax import lax
from jax.experimental import pallas as pl
from jax.experimental.pallas import tpu as pltpu
from jax.sharding import PartitionSpec as P

MESH = pl.DeviceIdType.MESH
F32 = jnp.float32
BF16 = jnp.bfloat16
B = 128
E = 384
NX, NY, NZ = 4, 4, 8
ROWS = NZ * 2 * B
COLS = NX * NY * B
R2 = 2 * B
LOG2E = math.log2(math.e)
LN2 = math.log(2.0)


def nt(a, b):
    return lax.dot_general(a, b, (((1,), (1,)), ((), ())), preferred_element_type=F32)


def kernel(
    scale_ref, img_ref, txt_ref, loss_ref, gi_ref, gt_ref,
    img_all, txt_all, img_t, s_ref, w_ref,
    rm_ref, rl_ref, cm_ref, cl_ref, lrb_ref, lc_ref,
    msg_r, msg_c, got_r, got_c, out_a, out_b, got_a, got_b,
    keep_i, sib_out, sib_in, far_out, far_in, keep_t, t_out, t_in,
    is_s, is_r, fs_s, fs_r, ts_s, ts_r, mr_s, mr_r, mc_s, mc_r,
    la_s, la_r, lb_s, lb_r, sb_s, sb_r, fo_s, fo_r, to_s, to_r,
):
    outer, inner = lax.axis_index("outer"), lax.axis_index("inner")
    c = outer % 2
    x = (outer // 2) % NX
    y = (outer // (2 * NX)) * 2 + inner // NZ
    z = inner % NZ
    factor = scale_ref[0]
    f2 = factor * LOG2E

    def dev(dx, dy, dz, dc):
        xx, yy, zz = (x + dx + NX) % NX, (y + dy + NY) % NY, (z + dz + NZ) % NZ
        cc = (c + dc) % 2
        return ((yy // 2) * (2 * NX) + xx * 2 + cc, (yy % 2) * NZ + zz)

    def rcopy(src, dst, ss, rs, to):
        return pltpu.make_async_remote_copy(
            src_ref=src, dst_ref=dst, send_sem=ss, recv_sem=rs, device_id=to, device_id_type=MESH
        )

    barrier = pltpu.get_barrier_semaphore()
    row_peers = [(d, r) for d in range(NZ) for r in range(2) if (d, r) != (0, 0)]
    col_peers = [(i, j) for i in range(NX) for j in range(NY) if (i, j) != (0, 0)]
    for d, r in row_peers:
        pl.semaphore_signal(barrier, inc=1, device_id=dev(0, 0, d, r), device_id_type=MESH)
    for i, j in col_peers:
        pl.semaphore_signal(barrier, inc=1, device_id=dev(i, j, 0, 0), device_id_type=MESH)
    pl.semaphore_wait(barrier, len(row_peers) + len(col_peers))

    def img_copy(k):
        return rcopy(img_ref, img_all.at[pl.ds(k * R2, B)], is_s.at[k], is_r.at[k], dev(0, 0, k, 0))

    def sib_copy(k):
        return rcopy(
            img_all.at[pl.ds(k * R2, B)], img_all.at[pl.ds(k * R2 + B, B)], fs_s.at[k], fs_r.at[k], dev(0, 0, 0, 1)
        )

    def txt_copy(i, j):
        q = i * NY + j
        return rcopy(txt_ref, txt_all.at[pl.ds(q * B, B)], ts_s.at[q], ts_r.at[q], dev(i, j, 0, 0))

    img_all[0:B, :] = img_ref[...]
    txt_all[0:B, :] = txt_ref[...]
    sib_copy(0).start()
    for k in (1, 7, 2, 6, 3, 5, 4):
        img_copy(k).start()
    for i, j in col_peers:
        txt_copy(i, j).start()

    prod = img_ref[...].astype(F32) * txt_ref[...].astype(F32)
    prod = prod[:, 0:128] + prod[:, 128:256] + prod[:, 256:384]
    msg_r[16:24, :] = jnp.sum(prod.reshape(B // 8, 8, 128), 0)

    for i, j in col_peers:
        txt_copy(i, j).wait()

    def first_step(n, _):
        k = jnp.where(n % 2 == 1, (n + 1) // 2, (NZ - n // 2) % NZ)
        row0 = pl.multiple_of(k * R2, R2)

        @pl.when(n > 0)
        def _():
            img_copy(k).wait()
            sib_copy(k).start()

        sib_copy(k).wait()
        block = img_all[pl.ds(row0, R2), :]
        img_t[:, pl.ds(row0, R2)] = block.T
        for cc in range(COLS // 256):
            s = nt(block, txt_all[cc * 256 : (cc + 1) * 256, :]) * f2
            s_ref[pl.ds(row0, R2), cc * 256 : (cc + 1) * 256] = s
        for cc in range(COLS // 128):
            lanes = slice(cc * 128, (cc + 1) * 128)
            slab = s_ref[pl.ds(row0, R2), lanes].reshape(R2 // 8, 8, 128)
            top = jnp.max(slab, 0)
            cm_ref[k, :, lanes] = top
            cl_ref[k, :, lanes] = jnp.sum(jnp.exp2(slab - top[None]), 0)
        for rr in range(R2 // 16):
            rows = pl.ds(row0 + rr * 16, 16)
            parts = [s_ref[rows, cc * 128 : (cc + 1) * 128] for cc in range(COLS // 128)]
            top = parts[0]
            for p in parts[1:]:
                top = jnp.maximum(top, p)
            total = jnp.exp2(parts[0] - top)
            for p in parts[1:]:
                total = total + jnp.exp2(p - top)
            rm_ref[rr * 16 : rr * 16 + 16, :] = top
            rl_ref[rr * 16 : rr * 16 + 16, :] = total
        for r in range(2):
            mt = rm_ref[r * B : (r + 1) * B, :].T
            lt = rl_ref[r * B : (r + 1) * B, :].T
            top = jnp.max(mt, 0, keepdims=True)
            total = jnp.sum(lt * jnp.exp2(mt - top), 0, keepdims=True)
            msg_r[pl.ds(r * NZ + k, 1), :] = top + jnp.log(total) * LOG2E
        return 0

    lax.fori_loop(0, NZ, first_step, 0)

    for cc in range(COLS // 128):
        lanes = slice(cc * 128, (cc + 1) * 128)
        mt = cm_ref[:, :, lanes].reshape(NZ * 8, 128)
        lt = cl_ref[:, :, lanes].reshape(NZ * 8, 128)
        top = jnp.max(mt, 0, keepdims=True)
        total = jnp.sum(lt * jnp.exp2(mt - top), 0, keepdims=True)
        msg_c[cc : cc + 1, :] = top + jnp.log(total) * LOG2E

    def row_msg(d, r):
        q = d * 2 + r
        return rcopy(msg_r, got_r.at[q], mr_s.at[q], mr_r.at[q], dev(0, 0, d, r))

    def col_msg(i, j):
        q = i * NY + j
        return rcopy(msg_c, got_c.at[q], mc_s.at[q], mc_r.at[q], dev(i, j, 0, 0))

    for d, r in row_peers:
        row_msg(d, r).start()
    for i, j in col_peers:
        col_msg(i, j).start()

    def combine(parts):
        top = parts[0]
        for p in parts[1:]:
            top = jnp.maximum(top, p)
        total = jnp.exp2(parts[0] - top)
        for p in parts[1:]:
            total = total + jnp.exp2(p - top)
        return top + jnp.log(total) * LOG2E

    for d, r in row_peers:
        row_msg(d, r).wait()
    halves = ([], [])
    diag = msg_r[16:24, :]
    for d in range(NZ):
        for r in range(2):
            ref = msg_r if (d, r) == (0, 0) else got_r.at[d * 2 + r]
            if (d, r) != (0, 0):
                diag = diag + ref[16:24, :]
            for rs in range(2):
                v = ref[rs * 8 : rs * 8 + 8, :]
                halves[rs ^ r].append(pltpu.roll(v, d, 0) if d else v)
    lr = [combine(h) for h in halves]

    for i, j in col_peers:
        col_msg(i, j).wait()
    jj = lax.broadcasted_iota(jnp.int32, (NX * NY, 128), 0) % NY
    parts = []
    for a in range(NX):
        for b in range(NY):
            v = msg_c[...] if (a, b) == (0, 0) else got_c[a * NY + b]
            s1, s2 = (4 * a + b) % 16, (4 * a + b + 12) % 16
            if b == 0:
                v = pltpu.roll(v, s1, 0) if s1 else v
            else:
                v = jnp.where(jj >= b, pltpu.roll(v, s1, 0), pltpu.roll(v, s2, 0) if s2 else v)
            parts.append(v)
    lc = combine(parts)
    lc_ref[...] = lc + 1.0

    out_a[...] = (lr[0] + lr[1]) * LN2 - (2.0 * factor) * diag
    out_b[...] = (lc[0:8] + lc[8:16]) * LN2

    def a_msg(i, j):
        q = i * NY + j
        return rcopy(out_a, got_a.at[q], la_s.at[q], la_r.at[q], dev(i, j, 0, 0))

    def b_msg(d, r):
        q = d * 2 + r
        return rcopy(out_b, got_b.at[q], lb_s.at[q], lb_r.at[q], dev(0, 0, d, r))

    for i, j in col_peers:
        a_msg(i, j).start()
    for d, r in row_peers:
        b_msg(d, r).start()

    for k in range(NZ):
        for r in range(2):
            lrb_ref[k * R2 + r * B : k * R2 + (r + 1) * B, :] = (
                jnp.broadcast_to(lr[r][k : k + 1, :], (B, 128)) + 1.0
            ).T

    def order(n):
        return jnp.where(n % 2 == 0, NZ // 2 - n // 2, (NZ // 2 + (n + 1) // 2) % NZ)

    def sib_part(k):
        return rcopy(sib_out.at[k], sib_in.at[k], sb_s.at[k], sb_r.at[k], dev(0, 0, 0, 1))

    def far_part(k):
        return rcopy(far_out.at[k], far_in.at[k], fo_s.at[k], fo_r.at[k], dev(0, 0, -k, 0))

    def pass_on(k):
        sib_part(k).wait_recv()
        far_out[k] = (keep_i[k] + sib_in[k]).astype(BF16)
        far_part(k).start()

    def second_step(n, _):
        k = order(n)
        row0 = pl.multiple_of(k * R2, R2)
        rows = pl.ds(row0, R2)
        for cc in range(COLS // 128):
            lanes = slice(cc * 128, (cc + 1) * 128)
            s = s_ref[rows, lanes]
            w = jnp.exp2(s - lrb_ref[rows, :]) + jnp.exp2(s - lc_ref[cc : cc + 1, :])
            w_ref[rows, lanes] = w.astype(BF16)
        part = jnp.dot(w_ref[rows, :], txt_all[...], preferred_element_type=F32)
        keep_i[k] = part[0:B]
        sib_out[k] = part[B:R2]
        sib_part(k).start()

        @pl.when(n > 0)
        def _():
            pass_on(order(n - 1))

        return 0

    lax.fori_loop(0, NZ, second_step, 0)

    def txt_part(q):
        i, j = q // NY, q % NY
        return rcopy(t_out.at[q], t_in.at[q], to_s.at[q], to_r.at[q], dev(-i, -j, 0, 0))

    def third(cc):
        return jnp.dot(img_t[...], w_ref[:, pl.ds(pl.multiple_of(cc * 256, 256), 256)], preferred_element_type=F32)

    def third_step(n, _):
        cc = COLS // 256 - 1 - n
        part = third(cc)
        for h in range(2):
            t_out[2 * cc + h] = part[:, h * 128 : (h + 1) * 128].astype(BF16)
            txt_part(2 * cc + h).start()
        return 0

    lax.fori_loop(0, COLS // 256 - 1, third_step, 0)
    part = third(0)
    keep_t[...] = part[:, 0:128]
    t_out[1] = part[:, 128:256].astype(BF16)
    txt_part(1).start()

    sib_part(0).wait_recv()
    total = keep_i[0] + sib_in[0]
    for k in range(1, NZ):
        far_part(k).wait_recv()
        total = total + far_in[k].astype(F32)
    gi_ref[...] = factor * (total - txt_ref[...].astype(F32))

    for i, j in col_peers:
        a_msg(i, j).wait()
    for d, r in row_peers:
        b_msg(d, r).wait()
    share = out_a[...] + out_b[...]
    for q in range(1, 16):
        share = share + got_a[q] + got_b[q]
    loss_ref[0] = jnp.sum(share) / (2.0 * 256 * B)

    total = keep_t[...]
    for q in range(1, 16):
        txt_part(q).wait_recv()
        total = total + t_in[q].astype(F32)
    gt_ref[...] = factor * (total.T - img_ref[...].astype(F32))

    for k in range(NZ):
        sib_part(k).wait_send()
    for k in range(1, NZ):
        far_part(k).wait_send()
    for q in range(1, 16):
        txt_part(q).wait_send()


def local(images, texts, logit_scale):
    dma = pltpu.SemaphoreType.DMA
    vm = pltpu.VMEM
    return pl.pallas_call(
        kernel,
        out_shape=(
            jax.ShapeDtypeStruct((1,), F32),
            jax.ShapeDtypeStruct((B, E), F32),
            jax.ShapeDtypeStruct((B, E), F32),
        ),
        in_specs=[
            pl.BlockSpec(memory_space=pltpu.SMEM),
            pl.BlockSpec(memory_space=vm),
            pl.BlockSpec(memory_space=vm),
        ],
        out_specs=(
            pl.BlockSpec(memory_space=pltpu.SMEM),
            pl.BlockSpec(memory_space=vm),
            pl.BlockSpec(memory_space=vm),
        ),
        scratch_shapes=[
            vm((ROWS, E), BF16), vm((COLS, E), BF16), vm((E, ROWS), BF16),
            vm((ROWS, COLS), F32), vm((ROWS, COLS), BF16),
            vm((R2, 128), F32), vm((R2, 128), F32), vm((NZ, 8, COLS), F32), vm((NZ, 8, COLS), F32),
            vm((ROWS, 128), F32), vm((16, 128), F32),
            vm((24, 128), F32), vm((16, 128), F32), vm((16, 24, 128), F32), vm((16, 16, 128), F32),
            vm((8, 128), F32), vm((8, 128), F32), vm((16, 8, 128), F32), vm((16, 8, 128), F32),
            vm((NZ, B, E), F32), vm((NZ, B, E), F32), vm((NZ, B, E), F32),
            vm((NZ, B, E), BF16), vm((NZ, B, E), BF16),
            vm((E, B), F32), vm((16, E, B), BF16), vm((16, E, B), BF16),
            dma((NZ,)), dma((NZ,)), dma((NZ,)), dma((NZ,)), dma((16,)), dma((16,)),
            dma((16,)), dma((16,)), dma((16,)), dma((16,)),
            dma((16,)), dma((16,)), dma((16,)), dma((16,)),
            dma((NZ,)), dma((NZ,)), dma((NZ,)), dma((NZ,)), dma((16,)), dma((16,)),
        ],
        compiler_params=pltpu.CompilerParams(
            collective_id=0, has_side_effects=True, vmem_limit_bytes=56 * 1024 * 1024
        ),
        cost_estimate=pl.CostEstimate(
            flops=6 * ROWS * COLS * E, bytes_accessed=8 * B * E, transcendentals=4 * ROWS * COLS
        ),
    )(logit_scale, images, texts)


def solution(mesh):
    spec = P(("outer", "inner"), None)
    return jax.shard_map(
        local, mesh=mesh, in_specs=(spec, spec, P()), out_specs=(P(), spec, spec), check_vma=False
    )
```

time: 585 us -> 104 us (0.18)
  waiting for transfers between devices: 288 us -> 0 us
  blocking collectives: 175 us -> 0 us
  Pallas kernels: 0 us -> 97.6 us
  matrix products: 90.5 us -> 0 us
  between operations: 18.3 us -> 3.11 us
  other arithmetic: 9.33 us -> 0 us
    reduce_scatter x2 -> x0, waiting for transfers between devices: 158 us -> none  [the longest x1 88.4 us: local(): lax.psum_scatter(text_parts, 'outer', scatter_dimension=0, tiled=True)]
    all_gather x2 -> x0, waiting for transfers between devices: 127 us -> none  [the longest x1 65.7 us: local(): image_rows = lax.all_gather(images, 'inner', axis=0, tiled=True)]
    pallas_call x0 -> x1, Pallas kernels: none -> 97.6 us  [local(): pl.pallas_call(kernel, out_shape=(jax.ShapeDtypeStruct((1,), F32), jax.Sh...]
    all_gather x4 -> x0, blocking collectives: 91.9 us -> none  [merged(): pieces = jax.tree.map(lambda part: lax.all_gather(part, axis), value)]
    dot_general x32 -> x0, matrix products: 90.5 us -> none  [the longest x8 34.3 us: second_advance(): jnp.einsum('rc,re->ce', weights, block, preferred_element_type=jnp.float32)]
    psum x1 -> x0, blocking collectives: 83.3 us -> none  [local(): total_terms = lax.psum(local_terms, ('outer', 'inner'))]
    reduce_sum x10 -> x0, other arithmetic: 6.95 us -> none  [the longest x8 5.67 us: first_advance(): row_sum = jnp.sum(jnp.exp(score_tile - row_max[:, None]), 1)]
  transfers between devices with their start and end apart: 4 -> 0, of which waited for: 4 -> 0; matrix products, arithmetic and copies ran while one was open for 0% -> 0% of each run, Pallas kernels for 0% -> 0%
where the time goes in v1:
time: 104 us; the launch traced here: 103 us
  Pallas kernels  97.6 us (94%)
  between operations  3.11 us (3%)
  local copies, waits for them, and re-layouts  2.34 us (2%)
    pallas_call x1, Pallas kernels, local(): pl.pallas_call(kernel, out_shape=(jax.ShapeDtypeStruct((1,), F32), jax.Sh...  97.6 us
    unnamed x4, local copies, waits for them, and re-layouts  2.34 us

profile of v1, /device:TPU:1, one launch (start us, length us, event | category | flops | bytes accessed | tf_op | source)
XLA Modules:
  0.0 103.1 jit_solution(4988774940381826348)
XLA Ops:
  1.3 97.6 %shard_map.58 = (f32[1]{0:T(128)}, f32[128,384]{1,0:T(8,128)}, f32[128,384]{1,0:T(8,128)}) custom-call(f32[1]{0:T(128)S(6)} %copy.9.scale_ref, bf16[128,384]{1,0:T(8,128)(2,1)} %img_ref.1, bf16[128,384]{1,0:T(8,128)(2,1)} %txt_ref.1), custom_call_target="tpu_custom_call" | custom-call | flops 9663676416 | bytes 393216 | tf_op jit(solution)/shard_map/pallas_call | solution.py:304
  99.6 0.0 copy-start
  99.6 1.7 %copy.11 = f32[128,384]{1,0:T(8,128)} copy(f32[128,384]{1,0:T(8,128)} %get-tuple-element.7) | data formatting | bytes 393216
  101.2 0.0 copy-done
  101.3 0.7 copy.12
Async XLA Ops:
  99.6 1.7 %copy-start = (f32[128,384]{1,0:T(8,128)S(1)}, f32[128,384]{1,0:T(8,128)}, u32[]{:S(2)}) copy-start(f32[128,384]{1,0:T(8,128)} %get-tuple-element.8) | copy-start | bytes 589828

commit v2 on v1

--- a/solution.py
+++ b/solution.py
@@ -16,6 +16,7 @@
 ROWS = NZ * 2 * B
 COLS = NX * NY * B
 R2 = 2 * B
+QC = 4 * B
 LOG2E = math.log2(math.e)
 LN2 = math.log(2.0)
 
@@ -46,6 +47,9 @@
         cc = (c + dc) % 2
         return ((yy // 2) * (2 * NX) + xx * 2 + cc, (yy % 2) * NZ + zz)
 
+    def dev_ab(da, db):
+        return dev(jnp.where(c == 0, da, db), jnp.where(c == 0, db, da), 0, 0)
+
     def rcopy(src, dst, ss, rs, to):
         return pltpu.make_async_remote_copy(
             src_ref=src, dst_ref=dst, send_sem=ss, recv_sem=rs, device_id=to, device_id_type=MESH
@@ -57,77 +61,148 @@
     for d, r in row_peers:
         pl.semaphore_signal(barrier, inc=1, device_id=dev(0, 0, d, r), device_id_type=MESH)
     for i, j in col_peers:
-        pl.semaphore_signal(barrier, inc=1, device_id=dev(i, j, 0, 0), device_id_type=MESH)
+        pl.semaphore_signal(barrier, inc=1, device_id=dev_ab(i, j), device_id_type=MESH)
     pl.semaphore_wait(barrier, len(row_peers) + len(col_peers))
 
+    def img_rows(k, h=None):
+        return img_all.at[pl.ds(k * R2, B)] if h is None else img_all.at[pl.ds(k * R2 + h * 64, 64)]
+
     def img_copy(k):
-        return rcopy(img_ref, img_all.at[pl.ds(k * R2, B)], is_s.at[k], is_r.at[k], dev(0, 0, k, 0))
+        return rcopy(img_ref, img_rows(k), is_s.at[k], is_r.at[k], dev(0, 0, k, 0))
+
+    def img_forward(k, h=None):
+        if k == 3:
+            return rcopy(img_rows(2), img_rows(3), is_s.at[3], is_r.at[3], dev(0, 0, 1, 0))
+        if k == 5:
+            return rcopy(img_rows(6), img_rows(5), is_s.at[5], is_r.at[5], dev(0, 0, -1, 0))
+        if h == 0:
+            return rcopy(img_rows(2, 0), img_rows(4, 0), is_s.at[4], is_r.at[4], dev(0, 0, 2, 0))
+        return rcopy(img_rows(6, 1), img_rows(4, 1), is_s.at[8], is_r.at[8], dev(0, 0, -2, 0))
 
     def sib_copy(k):
+        return rcopy(img_rows(k), img_all.at[pl.ds(k * R2 + B, B)], fs_s.at[k], fs_r.at[k], dev(0, 0, 0, 1))
+
+    def txt_first(i):
+        return rcopy(txt_ref, txt_all.at[pl.ds(i * B, B)], ts_s.at[i], ts_r.at[i], dev_ab(i, 0))
+
+    def txt_second(j):
         return rcopy(
-            img_all.at[pl.ds(k * R2, B)], img_all.at[pl.ds(k * R2 + B, B)], fs_s.at[k], fs_r.at[k], dev(0, 0, 0, 1)
+            txt_all.at[pl.ds(0, QC)], txt_all.at[pl.ds(j * QC, QC)], ts_s.at[3 + j], ts_r.at[3 + j], dev_ab(0, j)
         )
-
-    def txt_copy(i, j):
-        q = i * NY + j
-        return rcopy(txt_ref, txt_all.at[pl.ds(q * B, B)], ts_s.at[q], ts_r.at[q], dev(i, j, 0, 0))
 
     img_all[0:B, :] = img_ref[...]
     txt_all[0:B, :] = txt_ref[...]
+    for i in (1, 3, 2):
+        txt_first(i).start()
+    for k in (2, 6, 1, 7):
+        img_copy(k).start()
     sib_copy(0).start()
-    for k in (1, 7, 2, 6, 3, 5, 4):
-        img_copy(k).start()
-    for i, j in col_peers:
-        txt_copy(i, j).start()
 
     prod = img_ref[...].astype(F32) * txt_ref[...].astype(F32)
     prod = prod[:, 0:128] + prod[:, 128:256] + prod[:, 256:384]
     msg_r[16:24, :] = jnp.sum(prod.reshape(B // 8, 8, 128), 0)
 
-    for i, j in col_peers:
-        txt_copy(i, j).wait()
-
-    def first_step(n, _):
-        k = jnp.where(n % 2 == 1, (n + 1) // 2, (NZ - n // 2) % NZ)
+    def near(n):
+        return jnp.where(n % 2 == 1, (n + 1) // 2, (NZ - n // 2) % NZ)
+
+    def tile(k, j):
         row0 = pl.multiple_of(k * R2, R2)
-
-        @pl.when(n > 0)
-        def _():
-            img_copy(k).wait()
-            sib_copy(k).start()
-
-        sib_copy(k).wait()
         block = img_all[pl.ds(row0, R2), :]
-        img_t[:, pl.ds(row0, R2)] = block.T
-        for cc in range(COLS // 256):
+        for cc in range(j * 2, j * 2 + 2):
             s = nt(block, txt_all[cc * 256 : (cc + 1) * 256, :]) * f2
             s_ref[pl.ds(row0, R2), cc * 256 : (cc + 1) * 256] = s
-        for cc in range(COLS // 128):
+        for cc in range(j * 4, j * 4 + 4):
             lanes = slice(cc * 128, (cc + 1) * 128)
             slab = s_ref[pl.ds(row0, R2), lanes].reshape(R2 // 8, 8, 128)
             top = jnp.max(slab, 0)
             cm_ref[k, :, lanes] = top
             cl_ref[k, :, lanes] = jnp.sum(jnp.exp2(slab - top[None]), 0)
-        for rr in range(R2 // 16):
-            rows = pl.ds(row0 + rr * 16, 16)
-            parts = [s_ref[rows, cc * 128 : (cc + 1) * 128] for cc in range(COLS // 128)]
-            top = parts[0]
-            for p in parts[1:]:
-                top = jnp.maximum(top, p)
-            total = jnp.exp2(parts[0] - top)
-            for p in parts[1:]:
-                total = total + jnp.exp2(p - top)
-            rm_ref[rr * 16 : rr * 16 + 16, :] = top
-            rl_ref[rr * 16 : rr * 16 + 16, :] = total
+        for rr in range(R2 // 32):
+            rows = pl.ds(row0 + rr * 32, 32)
+            parts = [s_ref[rows, cc * 128 : (cc + 1) * 128] for cc in range(j * 4, j * 4 + 4)]
+            top = jnp.maximum(jnp.maximum(parts[0], parts[1]), jnp.maximum(parts[2], parts[3]))
+            e = [jnp.exp2(p - top) for p in parts]
+            rm_ref[j, rows, :] = top
+            rl_ref[j, rows, :] = (e[0] + e[1]) + (e[2] + e[3])
+
+    def tiles(lo, hi, js, extra=None):
+        def step(n, _):
+            k = near(n)
+            for j in js:
+                tile(k, j)
+            if extra is not None:
+                extra(k)
+            return 0
+
+        lax.fori_loop(lo, hi, step, 0)
+
+    def turn(k):
+        row0 = pl.multiple_of(k * R2, R2)
+        img_t[:, pl.ds(row0, R2)] = img_all[pl.ds(row0, R2), :].T
+
+    def finish_rows(k):
         for r in range(2):
-            mt = rm_ref[r * B : (r + 1) * B, :].T
-            lt = rl_ref[r * B : (r + 1) * B, :].T
+            rows = pl.ds(pl.multiple_of(k * R2 + r * B, B), B)
+            top = jnp.maximum(
+                jnp.maximum(rm_ref[0, rows, :], rm_ref[1, rows, :]), jnp.maximum(rm_ref[2, rows, :], rm_ref[3, rows, :])
+            )
+            total = rl_ref[0, rows, :] * jnp.exp2(rm_ref[0, rows, :] - top)
+            for j in range(1, 4):
+                total = total + rl_ref[j, rows, :] * jnp.exp2(rm_ref[j, rows, :] - top)
+            mt, lt = top.T, total.T
             top = jnp.max(mt, 0, keepdims=True)
             total = jnp.sum(lt * jnp.exp2(mt - top), 0, keepdims=True)
             msg_r[pl.ds(r * NZ + k, 1), :] = top + jnp.log(total) * LOG2E
-        return 0
-
-    lax.fori_loop(0, NZ, first_step, 0)
+
+    for i in (1, 3, 2):
+        txt_first(i).wait_recv()
+    for j in (1, 3, 2):
+        txt_second(j).start()
+    for k in (1, 7):
+        img_copy(k).wait_recv()
+        sib_copy(k).start()
+    sib_copy(0).wait_recv()
+    tiles(0, 1, (0,), turn)
+    for k in (2, 6):
+        img_copy(k).wait_recv()
+    img_forward(3).start()
+    img_forward(5).start()
+    img_forward(4, 0).start()
+    img_forward(4, 1).start()
+    for k in (2, 6):
+        sib_copy(k).start()
+    for k in (1, 7, 2, 6):
+        sib_copy(k).wait_recv()
+    tiles(1, 5, (0,), turn)
+    txt_second(1).wait_recv()
+    tiles(0, 5, (1,))
+    img_forward(3).wait_recv()
+    img_forward(5).wait_recv()
+    sib_copy(3).start()
+    sib_copy(5).start()
+    txt_second(3).wait_recv()
+    tiles(0, 5, (3,))
+    img_forward(4, 0).wait_recv()
+    img_forward(4, 1).wait_recv()
+    sib_copy(4).start()
+    for k in (3, 5):
+        sib_copy(k).wait_recv()
+    tiles(5, 7, (0, 1, 3), turn)
+    sib_copy(4).wait_recv()
+    tiles(7, 8, (0, 1, 3), turn)
+    txt_second(2).wait_recv()
+    tiles(0, 8, (2,), finish_rows)
+
+    for i in (1, 3, 2):
+        txt_first(i).wait_send()
+    for j in (1, 3, 2):
+        txt_second(j).wait_send()
+    for k in (1, 2, 6, 7):
+        img_copy(k).wait_send()
+    for k, h in ((3, None), (5, None), (4, 0), (4, 1)):
+        img_forward(k, h).wait_send()
+    for k in range(NZ):
+        sib_copy(k).wait_send()
 
     for cc in range(COLS // 128):
         lanes = slice(cc * 128, (cc + 1) * 128)
@@ -142,8 +217,8 @@
         return rcopy(msg_r, got_r.at[q], mr_s.at[q], mr_r.at[q], dev(0, 0, d, r))
 
     def col_msg(i, j):
-        q = i * NY + j
-        return rcopy(msg_c, got_c.at[q], mc_s.at[q], mc_r.at[q], dev(i, j, 0, 0))
+        q = j * 4 + i
+        return rcopy(msg_c, got_c.at[q], mc_s.at[q], mc_r.at[q], dev_ab(i, j))
 
     for d, r in row_peers:
         row_msg(d, r).start()
@@ -193,8 +268,8 @@
     out_b[...] = (lc[0:8] + lc[8:16]) * LN2
 
     def a_msg(i, j):
-        q = i * NY + j
-        return rcopy(out_a, got_a.at[q], la_s.at[q], la_r.at[q], dev(i, j, 0, 0))
+        q = j * 4 + i
+        return rcopy(out_a, got_a.at[q], la_s.at[q], la_r.at[q], dev_ab(i, j))
 
     def b_msg(d, r):
         q = d * 2 + r
@@ -248,8 +323,7 @@
     lax.fori_loop(0, NZ, second_step, 0)
 
     def txt_part(q):
-        i, j = q // NY, q % NY
-        return rcopy(t_out.at[q], t_in.at[q], to_s.at[q], to_r.at[q], dev(-i, -j, 0, 0))
+        return rcopy(t_out.at[q], t_in.at[q], to_s.at[q], to_r.at[q], dev_ab(-(q % 4), -(q // 4)))
 
     def third(cc):
         return jnp.dot(img_t[...], w_ref[:, pl.ds(pl.multiple_of(cc * 256, 256), 256)], preferred_element_type=F32)
@@ -321,14 +395,14 @@
         scratch_shapes=[
             vm((ROWS, E), BF16), vm((COLS, E), BF16), vm((E, ROWS), BF16),
             vm((ROWS, COLS), F32), vm((ROWS, COLS), BF16),
-            vm((R2, 128), F32), vm((R2, 128), F32), vm((NZ, 8, COLS), F32), vm((NZ, 8, COLS), F32),
+            vm((4, ROWS, 128), F32), vm((4, ROWS, 128), F32), vm((NZ, 8, COLS), F32), vm((NZ, 8, COLS), F32),
             vm((ROWS, 128), F32), vm((16, 128), F32),
             vm((24, 128), F32), vm((16, 128), F32), vm((16, 24, 128), F32), vm((16, 16, 128), F32),
             vm((8, 128), F32), vm((8, 128), F32), vm((16, 8, 128), F32), vm((16, 8, 128), F32),
             vm((NZ, B, E), F32), vm((NZ, B, E), F32), vm((NZ, B, E), F32),
             vm((NZ, B, E), BF16), vm((NZ, B, E), BF16),
             vm((E, B), F32), vm((16, E, B), BF16), vm((16, E, B), BF16),
-            dma((NZ,)), dma((NZ,)), dma((NZ,)), dma((NZ,)), dma((16,)), dma((16,)),
+            dma((9,)), dma((9,)), dma((NZ,)), dma((NZ,)), dma((16,)), dma((16,)),
             dma((16,)), dma((16,)), dma((16,)), dma((16,)),
             dma((16,)), dma((16,)), dma((16,)), dma((16,)),
             dma((NZ,)), dma((NZ,)), dma((NZ,)), dma((NZ,)), dma((16,)), dma((16,)),

time: 104 us -> 83.9 us (0.81)
  Pallas kernels: 97.6 us -> 78.3 us
    pallas_call x1, Pallas kernels: 97.6 us -> 78.3 us  [local(): pl.pallas_call(kernel, out_shape=(jax.ShapeDtypeStruct((1,), F32), jax.Sh...]
where the time goes in v2:
time: 83.9 us; the launch traced here: 83.8 us
  Pallas kernels  78.3 us (93%)
  between operations  3.11 us (4%)
  local copies, waits for them, and re-layouts  2.34 us (3%)
    pallas_call x1, Pallas kernels, local(): pl.pallas_call(kernel, out_shape=(jax.ShapeDtypeStruct((1,), F32), jax.Sh...  78.3 us
    unnamed x4, local copies, waits for them, and re-layouts  2.34 us

profile of v2, /device:TPU:1, one launch (start us, length us, event | category | flops | bytes accessed | tf_op | source)
XLA Modules:
  0.0 83.8 jit_solution(6372557879482812132)
XLA Ops:
  1.3 78.3 %shard_map.58 = (f32[1]{0:T(128)}, f32[128,384]{1,0:T(8,128)}, f32[128,384]{1,0:T(8,128)}) custom-call(f32[1]{0:T(128)S(6)} %copy.9.scale_ref, bf16[128,384]{1,0:T(8,128)(2,1)} %img_ref.1, bf16[128,384]{1,0:T(8,128)(2,1)} %txt_ref.1), custom_call_target="tpu_custom_call" | custom-call | flops 9663676416 | bytes 393216 | tf_op jit(solution)/shard_map/pallas_call | solution.py:378
  80.3 0.0 copy-start
  80.3 1.7 %copy.11 = f32[128,384]{1,0:T(8,128)} copy(f32[128,384]{1,0:T(8,128)} %get-tuple-element.7) | data formatting | bytes 393216
  81.9 0.0 copy-done
  82.0 0.7 copy.12
Async XLA Ops:
  80.3 1.7 %copy-start = (f32[128,384]{1,0:T(8,128)S(1)}, f32[128,384]{1,0:T(8,128)}, u32[]{:S(2)}) copy-start(f32[128,384]{1,0:T(8,128)} %get-tuple-element.8) | copy-start | bytes 589828

commit v3 on v2

--- a/solution.py
+++ b/solution.py
@@ -30,7 +30,7 @@
     img_all, txt_all, img_t, s_ref, w_ref,
     rm_ref, rl_ref, cm_ref, cl_ref, lrb_ref, lc_ref,
     msg_r, msg_c, got_r, got_c, out_a, out_b, got_a, got_b,
-    keep_i, sib_out, sib_in, far_out, far_in, keep_t, t_out, t_in,
+    keep_i, sib_out, sib_in, far_out, far_in, mid_in, keep_t, t_out, t_in, u_out, u_in,
     is_s, is_r, fs_s, fs_r, ts_s, ts_r, mr_s, mr_r, mc_s, mc_r,
     la_s, la_r, lb_s, lb_r, sb_s, sb_r, fo_s, fo_r, to_s, to_r,
 ):
@@ -286,68 +286,79 @@
                 jnp.broadcast_to(lr[r][k : k + 1, :], (B, 128)) + 1.0
             ).T
 
-    def order(n):
-        return jnp.where(n % 2 == 0, NZ // 2 - n // 2, (NZ // 2 + (n + 1) // 2) % NZ)
-
     def sib_part(k):
         return rcopy(sib_out.at[k], sib_in.at[k], sb_s.at[k], sb_r.at[k], dev(0, 0, 0, 1))
 
     def far_part(k):
+        if k == 3:
+            return rcopy(far_out.at[3], mid_in.at[0], fo_s.at[3], fo_r.at[3], dev(0, 0, -1, 0))
+        if k == 5:
+            return rcopy(far_out.at[5], mid_in.at[1], fo_s.at[5], fo_r.at[5], dev(0, 0, 1, 0))
+        if k == 4:
+            rows = pl.ds(0, 64)
+            return rcopy(far_out.at[4, rows], mid_in.at[2, rows], fo_s.at[4], fo_r.at[4], dev(0, 0, -2, 0))
+        if k == 8:
+            rows = pl.ds(64, 64)
+            return rcopy(far_out.at[4, rows], mid_in.at[2, rows], fo_s.at[8], fo_r.at[8], dev(0, 0, 2, 0))
         return rcopy(far_out.at[k], far_in.at[k], fo_s.at[k], fo_r.at[k], dev(0, 0, -k, 0))
 
     def pass_on(k):
         sib_part(k).wait_recv()
-        far_out[k] = (keep_i[k] + sib_in[k]).astype(BF16)
+        total = keep_i[k] + sib_in[k]
+        if k in (2, 6):
+            half = 0 if k == 2 else 1
+            far_part(3 if k == 2 else 5).wait_recv()
+            far_part(4 if k == 2 else 8).wait_recv()
+            total = total + mid_in[half].astype(F32)
+            h = slice(half * 64, half * 64 + 64)
+            far_out[k] = total.astype(BF16)
+            far_out[k, h, :] = (total[h] + mid_in[2, h, :].astype(F32)).astype(BF16)
+        else:
+            far_out[k] = total.astype(BF16)
         far_part(k).start()
-
-    def second_step(n, _):
-        k = order(n)
+        if k == 4:
+            far_part(8).start()
+
+    def weigh(k, js):
         row0 = pl.multiple_of(k * R2, R2)
         rows = pl.ds(row0, R2)
-        for cc in range(COLS // 128):
-            lanes = slice(cc * 128, (cc + 1) * 128)
-            s = s_ref[rows, lanes]
-            w = jnp.exp2(s - lrb_ref[rows, :]) + jnp.exp2(s - lc_ref[cc : cc + 1, :])
-            w_ref[rows, lanes] = w.astype(BF16)
-        part = jnp.dot(w_ref[rows, :], txt_all[...], preferred_element_type=F32)
+        for j in js:
+            for cc in range(j * 4, j * 4 + 4):
+                lanes = slice(cc * 128, (cc + 1) * 128)
+                s = s_ref[rows, lanes]
+                w = jnp.exp2(s - lrb_ref[rows, :]) + jnp.exp2(s - lc_ref[cc : cc + 1, :])
+                w_ref[rows, lanes] = w.astype(BF16)
+
+    def txt_part(j):
+        return rcopy(t_out.at[j], t_in.at[j], to_s.at[j], to_r.at[j], dev_ab(0, -j))
+
+    def txt_part2(i):
+        return rcopy(u_out.at[i], u_in.at[i], to_s.at[4 + i], to_r.at[4 + i], dev_ab(-i, 0))
+
+    def third(j):
+        return jnp.dot(img_t[...], w_ref[:, j * QC : (j + 1) * QC], preferred_element_type=F32)
+
+    def send_quarter(j):
+        t_out[j] = third(j).astype(BF16)
+        txt_part(j).start()
+
+    for j in (2, 1):
+        lax.fori_loop(0, NZ, lambda k, t, j=j: (weigh(k, (j,)), t)[1], 0)
+        send_quarter(j)
+
+    ks = (4, 3, 5, 1, 7, 2, 6, 0)
+    for n, k in enumerate(ks):
+        weigh(k, (0, 3))
+        part = jnp.dot(w_ref[k * R2 : (k + 1) * R2, :], txt_all[...], preferred_element_type=F32)
         keep_i[k] = part[0:B]
         sib_out[k] = part[B:R2]
         sib_part(k).start()
-
-        @pl.when(n > 0)
-        def _():
-            pass_on(order(n - 1))
-
-        return 0
-
-    lax.fori_loop(0, NZ, second_step, 0)
-
-    def txt_part(q):
-        return rcopy(t_out.at[q], t_in.at[q], to_s.at[q], to_r.at[q], dev_ab(-(q % 4), -(q // 4)))
-
-    def third(cc):
-        return jnp.dot(img_t[...], w_ref[:, pl.ds(pl.multiple_of(cc * 256, 256), 256)], preferred_element_type=F32)
-
-    def third_step(n, _):
-        cc = COLS // 256 - 1 - n
-        part = third(cc)
-        for h in range(2):
-            t_out[2 * cc + h] = part[:, h * 128 : (h + 1) * 128].astype(BF16)
-            txt_part(2 * cc + h).start()
-        return 0
-
-    lax.fori_loop(0, COLS // 256 - 1, third_step, 0)
-    part = third(0)
-    keep_t[...] = part[:, 0:128]
-    t_out[1] = part[:, 128:256].astype(BF16)
-    txt_part(1).start()
-
-    sib_part(0).wait_recv()
-    total = keep_i[0] + sib_in[0]
-    for k in range(1, NZ):
-        far_part(k).wait_recv()
-        total = total + far_in[k].astype(F32)
-    gi_ref[...] = factor * (total - txt_ref[...].astype(F32))
+        if 1 <= n <= 5:
+            pass_on(ks[n - 1])
+    send_quarter(3)
+    pass_on(2)
+    pass_on(6)
+    keep_t[...] = third(0)
 
     for i, j in col_peers:
         a_msg(i, j).wait()
@@ -358,18 +369,36 @@
         share = share + got_a[q] + got_b[q]
     loss_ref[0] = jnp.sum(share) / (2.0 * 256 * B)
 
-    total = keep_t[...]
-    for q in range(1, 16):
-        txt_part(q).wait_recv()
-        total = total + t_in[q].astype(F32)
-    gt_ref[...] = factor * (total.T - img_ref[...].astype(F32))
+    for j in (2, 1, 3):
+        txt_part(j).wait_recv()
+    for i in (2, 1, 3, 0):
+        h = slice(i * B, (i + 1) * B)
+        total = keep_t[:, h] + t_in[1, :, h].astype(F32) + t_in[2, :, h].astype(F32) + t_in[3, :, h].astype(F32)
+        if i:
+            u_out[i] = total.astype(BF16)
+            txt_part2(i).start()
+        else:
+            own_t = total
+
+    sib_part(0).wait_recv()
+    total = keep_i[0] + sib_in[0]
+    for k in (1, 7, 2, 6):
+        far_part(k).wait_recv()
+        total = total + far_in[k].astype(F32)
+    gi_ref[...] = factor * (total - txt_ref[...].astype(F32))
+
+    for i in (1, 3, 2):
+        txt_part2(i).wait_recv()
+        own_t = own_t + u_in[i].astype(F32)
+    gt_ref[...] = factor * (own_t.T - img_ref[...].astype(F32))
 
     for k in range(NZ):
         sib_part(k).wait_send()
-    for k in range(1, NZ):
+    for k in range(1, NZ + 1):
         far_part(k).wait_send()
-    for q in range(1, 16):
-        txt_part(q).wait_send()
+    for j in range(1, 4):
+        txt_part(j).wait_send()
+        txt_part2(j).wait_send()
 
 
 def local(images, texts, logit_scale):
@@ -400,12 +429,12 @@
             vm((24, 128), F32), vm((16, 128), F32), vm((16, 24, 128), F32), vm((16, 16, 128), F32),
             vm((8, 128), F32), vm((8, 128), F32), vm((16, 8, 128), F32), vm((16, 8, 128), F32),
             vm((NZ, B, E), F32), vm((NZ, B, E), F32), vm((NZ, B, E), F32),
-            vm((NZ, B, E), BF16), vm((NZ, B, E), BF16),
-            vm((E, B), F32), vm((16, E, B), BF16), vm((16, E, B), BF16),
+            vm((NZ, B, E), BF16), vm((NZ, B, E), BF16), vm((3, B, E), BF16),
+            vm((E, QC), F32), vm((4, E, QC), BF16), vm((4, E, QC), BF16), vm((4, E, B), BF16), vm((4, E, B), BF16),
             dma((9,)), dma((9,)), dma((NZ,)), dma((NZ,)), dma((16,)), dma((16,)),
             dma((16,)), dma((16,)), dma((16,)), dma((16,)),
             dma((16,)), dma((16,)), dma((16,)), dma((16,)),
-            dma((NZ,)), dma((NZ,)), dma((NZ,)), dma((NZ,)), dma((16,)), dma((16,)),
+            dma((NZ,)), dma((NZ,)), dma((9,)), dma((9,)), dma((8,)), dma((8,)),
         ],
         compiler_params=pltpu.CompilerParams(
             collective_id=0, has_side_effects=True, vmem_limit_bytes=56 * 1024 * 1024

time: 83.9 us -> 78.5 us (0.936)
  Pallas kernels: 78.3 us -> 72.9 us
    pallas_call x1, Pallas kernels: 78.3 us -> 72.9 us  [local(): pl.pallas_call(kernel, out_shape=(jax.ShapeDtypeStruct((1,), F32), jax.Sh...]
where the time goes in v3:
time: 78.5 us; the launch traced here: 78.4 us
  Pallas kernels  72.9 us (93%)
  between operations  3.11 us (4%)
  local copies, waits for them, and re-layouts  2.34 us (3%)
    pallas_call x1, Pallas kernels, local(): pl.pallas_call(kernel, out_shape=(jax.ShapeDtypeStruct((1,), F32), jax.Sh...  72.9 us
    unnamed x4, local copies, waits for them, and re-layouts  2.34 us

profile of v3, /device:TPU:1, one launch (start us, length us, event | category | flops | bytes accessed | tf_op | source)
XLA Modules:
  0.0 78.4 jit_solution(18131978993443059827)
XLA Ops:
  1.3 72.9 %shard_map.58 = (f32[1]{0:T(128)}, f32[128,384]{1,0:T(8,128)}, f32[128,384]{1,0:T(8,128)}) custom-call(f32[1]{0:T(128)S(6)} %copy.9.scale_ref, bf16[128,384]{1,0:T(8,128)(2,1)} %img_ref.1, bf16[128,384]{1,0:T(8,128)(2,1)} %txt_ref.1), custom_call_target="tpu_custom_call" | custom-call | flops 9663676416 | bytes 393216 | tf_op jit(solution)/shard_map/pallas_call | solution.py:407
  74.9 0.0 copy-start
  74.9 1.7 %copy.11 = f32[128,384]{1,0:T(8,128)} copy(f32[128,384]{1,0:T(8,128)} %get-tuple-element.7) | data formatting | bytes 393216
  76.5 0.0 copy-done
  76.5 0.7 copy.12
Async XLA Ops:
  74.9 1.7 %copy-start = (f32[128,384]{1,0:T(8,128)S(1)}, f32[128,384]{1,0:T(8,128)}, u32[]{:S(2)}) copy-start(f32[128,384]{1,0:T(8,128)} %get-tuple-element.8) | copy-start | bytes 589828

commit v4 on v3

--- a/solution.py
+++ b/solution.py
@@ -32,7 +32,7 @@
     msg_r, msg_c, got_r, got_c, out_a, out_b, got_a, got_b,
     keep_i, sib_out, sib_in, far_out, far_in, mid_in, keep_t, t_out, t_in, u_out, u_in,
     is_s, is_r, fs_s, fs_r, ts_s, ts_r, mr_s, mr_r, mc_s, mc_r,
-    la_s, la_r, lb_s, lb_r, sb_s, sb_r, fo_s, fo_r, to_s, to_r,
+    la_s, la_r, lb_s, lb_r, sb_s, sb_r, fo_s, fo_r, to_s, uo_s, to_r,
 ):
     outer, inner = lax.axis_index("outer"), lax.axis_index("inner")
     c = outer % 2
@@ -55,6 +55,9 @@
             src_ref=src, dst_ref=dst, send_sem=ss, recv_sem=rs, device_id=to, device_id_type=MESH
         )
 
+    def drain(ref, sem):
+        pltpu.make_async_copy(ref, ref, sem).wait()
+
     barrier = pltpu.get_barrier_semaphore()
     row_peers = [(d, r) for d in range(NZ) for r in range(2) if (d, r) != (0, 0)]
     col_peers = [(i, j) for i in range(NX) for j in range(NY) if (i, j) != (0, 0)]
@@ -68,27 +71,30 @@
         return img_all.at[pl.ds(k * R2, B)] if h is None else img_all.at[pl.ds(k * R2 + h * 64, 64)]
 
     def img_copy(k):
-        return rcopy(img_ref, img_rows(k), is_s.at[k], is_r.at[k], dev(0, 0, k, 0))
+        return rcopy(img_ref, img_rows(k), is_s, is_r.at[k], dev(0, 0, k, 0))
 
     def img_forward(k, h=None):
         if k == 3:
-            return rcopy(img_rows(2), img_rows(3), is_s.at[3], is_r.at[3], dev(0, 0, 1, 0))
+            return rcopy(img_rows(2), img_rows(3), is_s, is_r.at[3], dev(0, 0, 1, 0))
         if k == 5:
-            return rcopy(img_rows(6), img_rows(5), is_s.at[5], is_r.at[5], dev(0, 0, -1, 0))
+            return rcopy(img_rows(6), img_rows(5), is_s, is_r.at[5], dev(0, 0, -1, 0))
         if h == 0:
-            return rcopy(img_rows(2, 0), img_rows(4, 0), is_s.at[4], is_r.at[4], dev(0, 0, 2, 0))
-        return rcopy(img_rows(6, 1), img_rows(4, 1), is_s.at[8], is_r.at[8], dev(0, 0, -2, 0))
+            return rcopy(img_rows(2, 0), img_rows(4, 0), is_s, is_r.at[4], dev(0, 0, 2, 0))
+        return rcopy(img_rows(6, 1), img_rows(4, 1), is_s, is_r.at[8], dev(0, 0, -2, 0))
 
     def sib_copy(k):
-        return rcopy(img_rows(k), img_all.at[pl.ds(k * R2 + B, B)], fs_s.at[k], fs_r.at[k], dev(0, 0, 0, 1))
+        return rcopy(img_rows(k), img_all.at[pl.ds(k * R2 + B, B)], fs_s, fs_r.at[k], dev(0, 0, 0, 1))
 
     def txt_first(i):
-        return rcopy(txt_ref, txt_all.at[pl.ds(i * B, B)], ts_s.at[i], ts_r.at[i], dev_ab(i, 0))
-
-    def txt_second(j):
+        return rcopy(txt_ref, txt_all.at[pl.ds(i * B, B)], ts_s, ts_r.at[i], dev_ab(i, 0))
+
+    def txt_second(i, j):
         return rcopy(
-            txt_all.at[pl.ds(0, QC)], txt_all.at[pl.ds(j * QC, QC)], ts_s.at[3 + j], ts_r.at[3 + j], dev_ab(0, j)
+            txt_all.at[pl.ds(i * B, B)], txt_all.at[pl.ds((j * 4 + i) * B, B)], ts_s, ts_r.at[3 + j], dev_ab(0, j)
         )
+
+    def txt_quarter(j):
+        drain(txt_all.at[pl.ds(j * QC, QC)], ts_r.at[3 + j])
 
     img_all[0:B, :] = img_ref[...]
     txt_all[0:B, :] = txt_ref[...]
@@ -96,113 +102,99 @@
         txt_first(i).start()
     for k in (2, 6, 1, 7):
         img_copy(k).start()
+    for j in (1, 3, 2):
+        txt_second(0, j).start()
     sib_copy(0).start()
 
     prod = img_ref[...].astype(F32) * txt_ref[...].astype(F32)
     prod = prod[:, 0:128] + prod[:, 128:256] + prod[:, 256:384]
     msg_r[16:24, :] = jnp.sum(prod.reshape(B // 8, 8, 128), 0)
 
-    def near(n):
-        return jnp.where(n % 2 == 1, (n + 1) // 2, (NZ - n // 2) % NZ)
-
     def tile(k, j):
-        row0 = pl.multiple_of(k * R2, R2)
-        block = img_all[pl.ds(row0, R2), :]
+        row0 = k * R2
+        block = img_all[row0 : row0 + R2, :]
         for cc in range(j * 2, j * 2 + 2):
             s = nt(block, txt_all[cc * 256 : (cc + 1) * 256, :]) * f2
-            s_ref[pl.ds(row0, R2), cc * 256 : (cc + 1) * 256] = s
+            s_ref[row0 : row0 + R2, cc * 256 : (cc + 1) * 256] = s
         for cc in range(j * 4, j * 4 + 4):
             lanes = slice(cc * 128, (cc + 1) * 128)
-            slab = s_ref[pl.ds(row0, R2), lanes].reshape(R2 // 8, 8, 128)
+            slab = s_ref[row0 : row0 + R2, lanes].reshape(R2 // 8, 8, 128)
             top = jnp.max(slab, 0)
             cm_ref[k, :, lanes] = top
             cl_ref[k, :, lanes] = jnp.sum(jnp.exp2(slab - top[None]), 0)
         for rr in range(R2 // 32):
-            rows = pl.ds(row0 + rr * 32, 32)
+            rows = slice(row0 + rr * 32, row0 + rr * 32 + 32)
             parts = [s_ref[rows, cc * 128 : (cc + 1) * 128] for cc in range(j * 4, j * 4 + 4)]
             top = jnp.maximum(jnp.maximum(parts[0], parts[1]), jnp.maximum(parts[2], parts[3]))
             e = [jnp.exp2(p - top) for p in parts]
             rm_ref[j, rows, :] = top
             rl_ref[j, rows, :] = (e[0] + e[1]) + (e[2] + e[3])
 
-    def tiles(lo, hi, js, extra=None):
-        def step(n, _):
-            k = near(n)
-            for j in js:
+    def tiles(ks, js):
+        for j in js:
+            for k in ks:
                 tile(k, j)
-            if extra is not None:
-                extra(k)
-            return 0
-
-        lax.fori_loop(lo, hi, step, 0)
 
     def turn(k):
-        row0 = pl.multiple_of(k * R2, R2)
-        img_t[:, pl.ds(row0, R2)] = img_all[pl.ds(row0, R2), :].T
+        img_t[:, k * R2 : (k + 1) * R2] = img_all[k * R2 : (k + 1) * R2, :].T
 
     def finish_rows(k):
         for r in range(2):
-            rows = pl.ds(pl.multiple_of(k * R2 + r * B, B), B)
-            top = jnp.maximum(
-                jnp.maximum(rm_ref[0, rows, :], rm_ref[1, rows, :]), jnp.maximum(rm_ref[2, rows, :], rm_ref[3, rows, :])
-            )
-            total = rl_ref[0, rows, :] * jnp.exp2(rm_ref[0, rows, :] - top)
-            for j in range(1, 4):
-                total = total + rl_ref[j, rows, :] * jnp.exp2(rm_ref[j, rows, :] - top)
-            mt, lt = top.T, total.T
-            top = jnp.max(mt, 0, keepdims=True)
-            total = jnp.sum(lt * jnp.exp2(mt - top), 0, keepdims=True)
-            msg_r[pl.ds(r * NZ + k, 1), :] = top + jnp.log(total) * LOG2E
+            rows = slice(k * R2 + r * B, k * R2 + r * B + B)
+            m = [rm_ref[j, rows, :] for j in range(4)]
+            top = jnp.maximum(jnp.maximum(m[0], m[1]), jnp.maximum(m[2], m[3]))
+            e = [rl_ref[j, rows, :] * jnp.exp2(m[j] - top) for j in range(4)]
+            v = (top + jnp.log((e[0] + e[1]) + (e[2] + e[3])) * LOG2E).T
+            top = jnp.max(v, 0, keepdims=True)
+            q = r * NZ + k
+            msg_r[q : q + 1, :] = top + jnp.log(jnp.sum(jnp.exp2(v - top), 0, keepdims=True)) * LOG2E
 
     for i in (1, 3, 2):
         txt_first(i).wait_recv()
-    for j in (1, 3, 2):
-        txt_second(j).start()
+        for j in (1, 3, 2):
+            txt_second(i, j).start()
+    sib_copy(0).wait_recv()
+    img_copy(2).wait_recv()
+    img_forward(3).start()
+    img_forward(4, 0).start()
+    img_copy(6).wait_recv()
+    img_forward(5).start()
+    img_forward(4, 1).start()
+    sib_copy(2).start()
+    sib_copy(6).start()
     for k in (1, 7):
         img_copy(k).wait_recv()
         sib_copy(k).start()
-    sib_copy(0).wait_recv()
-    tiles(0, 1, (0,), turn)
-    for k in (2, 6):
-        img_copy(k).wait_recv()
-    img_forward(3).start()
-    img_forward(5).start()
-    img_forward(4, 0).start()
-    img_forward(4, 1).start()
-    for k in (2, 6):
-        sib_copy(k).start()
-    for k in (1, 7, 2, 6):
+    tiles((0,), (0,))
+    turn(0)
+    for k in (2, 6, 1, 7):
         sib_copy(k).wait_recv()
-    tiles(1, 5, (0,), turn)
-    txt_second(1).wait_recv()
-    tiles(0, 5, (1,))
+    tiles((2, 6, 1, 7), (0,))
+    for k in (2, 6, 1, 7):
+        turn(k)
+    txt_quarter(1)
+    tiles((0, 2, 6, 1, 7), (1,))
     img_forward(3).wait_recv()
+    sib_copy(3).start()
     img_forward(5).wait_recv()
-    sib_copy(3).start()
     sib_copy(5).start()
-    txt_second(3).wait_recv()
-    tiles(0, 5, (3,))
+    txt_quarter(3)
+    tiles((0, 2, 6, 1, 7), (3,))
     img_forward(4, 0).wait_recv()
     img_forward(4, 1).wait_recv()
     sib_copy(4).start()
-    for k in (3, 5):
-        sib_copy(k).wait_recv()
-    tiles(5, 7, (0, 1, 3), turn)
+    sib_copy(3).wait_recv()
+    sib_copy(5).wait_recv()
+    tiles((3, 5), (0, 1, 3))
+    turn(3)
+    turn(5)
+    txt_quarter(2)
+    tiles((0, 2, 6, 1, 7, 3, 5), (2,))
     sib_copy(4).wait_recv()
-    tiles(7, 8, (0, 1, 3), turn)
-    txt_second(2).wait_recv()
-    tiles(0, 8, (2,), finish_rows)
-
-    for i in (1, 3, 2):
-        txt_first(i).wait_send()
-    for j in (1, 3, 2):
-        txt_second(j).wait_send()
-    for k in (1, 2, 6, 7):
-        img_copy(k).wait_send()
-    for k, h in ((3, None), (5, None), (4, 0), (4, 1)):
-        img_forward(k, h).wait_send()
+    tiles((4,), (0, 1, 3, 2))
+    turn(4)
     for k in range(NZ):
-        sib_copy(k).wait_send()
+        finish_rows(k)
 
     for cc in range(COLS // 128):
         lanes = slice(cc * 128, (cc + 1) * 128)
@@ -214,11 +206,11 @@
 
     def row_msg(d, r):
         q = d * 2 + r
-        return rcopy(msg_r, got_r.at[q], mr_s.at[q], mr_r.at[q], dev(0, 0, d, r))
+        return rcopy(msg_r, got_r.at[q], mr_s, mr_r, dev(0, 0, d, r))
 
     def col_msg(i, j):
         q = j * 4 + i
-        return rcopy(msg_c, got_c.at[q], mc_s.at[q], mc_r.at[q], dev_ab(i, j))
+        return rcopy(msg_c, got_c.at[q], mc_s, mc_r, dev_ab(i, j))
 
     for d, r in row_peers:
         row_msg(d, r).start()
@@ -234,8 +226,7 @@
             total = total + jnp.exp2(p - top)
         return top + jnp.log(total) * LOG2E
 
-    for d, r in row_peers:
-        row_msg(d, r).wait()
+    drain(got_r.at[pl.ds(1, 15)], mr_r)
     halves = ([], [])
     diag = msg_r[16:24, :]
     for d in range(NZ):
@@ -248,8 +239,7 @@
                 halves[rs ^ r].append(pltpu.roll(v, d, 0) if d else v)
     lr = [combine(h) for h in halves]
 
-    for i, j in col_peers:
-        col_msg(i, j).wait()
+    drain(got_c.at[pl.ds(1, 15)], mc_r)
     jj = lax.broadcasted_iota(jnp.int32, (NX * NY, 128), 0) % NY
     parts = []
     for a in range(NX):
@@ -269,11 +259,11 @@
 
     def a_msg(i, j):
         q = j * 4 + i
-        return rcopy(out_a, got_a.at[q], la_s.at[q], la_r.at[q], dev_ab(i, j))
+        return rcopy(out_a, got_a.at[q], la_s, la_r, dev_ab(i, j))
 
     def b_msg(d, r):
         q = d * 2 + r
-        return rcopy(out_b, got_b.at[q], lb_s.at[q], lb_r.at[q], dev(0, 0, d, r))
+        return rcopy(out_b, got_b.at[q], lb_s, lb_r, dev(0, 0, d, r))
 
     for i, j in col_peers:
         a_msg(i, j).start()
@@ -287,20 +277,20 @@
             ).T
 
     def sib_part(k):
-        return rcopy(sib_out.at[k], sib_in.at[k], sb_s.at[k], sb_r.at[k], dev(0, 0, 0, 1))
+        return rcopy(sib_out.at[k], sib_in.at[k], sb_s, sb_r.at[k], dev(0, 0, 0, 1))
 
     def far_part(k):
         if k == 3:
-            return rcopy(far_out.at[3], mid_in.at[0], fo_s.at[3], fo_r.at[3], dev(0, 0, -1, 0))
+            return rcopy(far_out.at[3], mid_in.at[0], fo_s, fo_r.at[3], dev(0, 0, -1, 0))
         if k == 5:
-            return rcopy(far_out.at[5], mid_in.at[1], fo_s.at[5], fo_r.at[5], dev(0, 0, 1, 0))
+            return rcopy(far_out.at[5], mid_in.at[1], fo_s, fo_r.at[5], dev(0, 0, 1, 0))
         if k == 4:
             rows = pl.ds(0, 64)
-            return rcopy(far_out.at[4, rows], mid_in.at[2, rows], fo_s.at[4], fo_r.at[4], dev(0, 0, -2, 0))
+            return rcopy(far_out.at[4, rows], mid_in.at[2, rows], fo_s, fo_r.at[4], dev(0, 0, -2, 0))
         if k == 8:
             rows = pl.ds(64, 64)
-            return rcopy(far_out.at[4, rows], mid_in.at[2, rows], fo_s.at[8], fo_r.at[8], dev(0, 0, 2, 0))
-        return rcopy(far_out.at[k], far_in.at[k], fo_s.at[k], fo_r.at[k], dev(0, 0, -k, 0))
+            return rcopy(far_out.at[4, rows], mid_in.at[2, rows], fo_s, fo_r.at[8], dev(0, 0, 2, 0))
+        return rcopy(far_out.at[k], far_in.at[k], fo_s, fo_r.at[k], dev(0, 0, -k, 0))
 
     def pass_on(k):
         sib_part(k).wait_recv()
@@ -320,8 +310,7 @@
             far_part(8).start()
 
     def weigh(k, js):
-        row0 = pl.multiple_of(k * R2, R2)
-        rows = pl.ds(row0, R2)
+        rows = slice(k * R2, (k + 1) * R2)
         for j in js:
             for cc in range(j * 4, j * 4 + 4):
                 lanes = slice(cc * 128, (cc + 1) * 128)
@@ -330,10 +319,10 @@
                 w_ref[rows, lanes] = w.astype(BF16)
 
     def txt_part(j):
-        return rcopy(t_out.at[j], t_in.at[j], to_s.at[j], to_r.at[j], dev_ab(0, -j))
+        return rcopy(t_out.at[j], t_in.at[j], to_s, to_r.at[j], dev_ab(0, -j))
 
     def txt_part2(i):
-        return rcopy(u_out.at[i], u_in.at[i], to_s.at[4 + i], to_r.at[4 + i], dev_ab(-i, 0))
+        return rcopy(u_out.at[i], u_in.at[i], uo_s, to_r.at[4 + i], dev_ab(-i, 0))
 
     def third(j):
         return jnp.dot(img_t[...], w_ref[:, j * QC : (j + 1) * QC], preferred_element_type=F32)
@@ -343,12 +332,15 @@
         txt_part(j).start()
 
     for j in (2, 1):
-        lax.fori_loop(0, NZ, lambda k, t, j=j: (weigh(k, (j,)), t)[1], 0)
+        for k in range(NZ):
+            weigh(k, (j,))
         send_quarter(j)
 
     ks = (4, 3, 5, 1, 7, 2, 6, 0)
+    weigh(ks[0], (0, 3))
     for n, k in enumerate(ks):
-        weigh(k, (0, 3))
+        if n < 7:
+            weigh(ks[n + 1], (0, 3))
         part = jnp.dot(w_ref[k * R2 : (k + 1) * R2, :], txt_all[...], preferred_element_type=F32)
         keep_i[k] = part[0:B]
         sib_out[k] = part[B:R2]
@@ -360,10 +352,8 @@
     pass_on(6)
     keep_t[...] = third(0)
 
-    for i, j in col_peers:
-        a_msg(i, j).wait()
-    for d, r in row_peers:
-        b_msg(d, r).wait()
+    drain(got_a.at[pl.ds(1, 15)], la_r)
+    drain(got_b.at[pl.ds(1, 15)], lb_r)
     share = out_a[...] + out_b[...]
     for q in range(1, 16):
         share = share + got_a[q] + got_b[q]
@@ -392,13 +382,17 @@
         own_t = own_t + u_in[i].astype(F32)
     gt_ref[...] = factor * (own_t.T - img_ref[...].astype(F32))
 
-    for k in range(NZ):
-        sib_part(k).wait_send()
-    for k in range(1, NZ + 1):
-        far_part(k).wait_send()
-    for j in range(1, 4):
-        txt_part(j).wait_send()
-        txt_part2(j).wait_send()
+    drain(txt_all.at[pl.ds(0, 15 * B)], ts_s)
+    drain(img_all.at[pl.ds(0, 7 * B)], is_s)
+    drain(img_all.at[pl.ds(0, 8 * B)], fs_s)
+    drain(got_r.at[pl.ds(1, 15)], mr_s)
+    drain(got_c.at[pl.ds(1, 15)], mc_s)
+    drain(got_a.at[pl.ds(1, 15)], la_s)
+    drain(got_b.at[pl.ds(1, 15)], lb_s)
+    drain(sib_in, sb_s)
+    drain(far_in.at[pl.ds(1, 7)], fo_s)
+    drain(t_in.at[pl.ds(1, 3)], to_s)
+    drain(u_in.at[pl.ds(1, 3)], uo_s)
 
 
 def local(images, texts, logit_scale):
@@ -431,10 +425,9 @@
             vm((NZ, B, E), F32), vm((NZ, B, E), F32), vm((NZ, B, E), F32),
             vm((NZ, B, E), BF16), vm((NZ, B, E), BF16), vm((3, B, E), BF16),
             vm((E, QC), F32), vm((4, E, QC), BF16), vm((4, E, QC), BF16), vm((4, E, B), BF16), vm((4, E, B), BF16),
-            dma((9,)), dma((9,)), dma((NZ,)), dma((NZ,)), dma((16,)), dma((16,)),
-            dma((16,)), dma((16,)), dma((16,)), dma((16,)),
-            dma((16,)), dma((16,)), dma((16,)), dma((16,)),
-            dma((NZ,)), dma((NZ,)), dma((9,)), dma((9,)), dma((8,)), dma((8,)),
+            dma, dma((9,)), dma, dma((NZ,)), dma, dma((7,)),
+            dma, dma, dma, dma, dma, dma, dma, dma,
+            dma, dma((NZ,)), dma, dma((9,)), dma, dma, dma((8,)),
         ],
         compiler_params=pltpu.CompilerParams(
             collective_id=0, has_side_effects=True, vmem_limit_bytes=56 * 1024 * 1024

time: 78.5 us -> 69.7 us (0.89)
  Pallas kernels: 72.9 us -> 64.1 us
    pallas_call x1, Pallas kernels: 72.9 us -> 64.1 us  [local(): pl.pallas_call(kernel, out_shape=(jax.ShapeDtypeStruct((1,), F32), jax.Sh...]
where the time goes in v4:
time: 69.7 us; the launch traced here: 69.6 us
  Pallas kernels  64.1 us (92%)
  between operations  3.11 us (4%)
  local copies, waits for them, and re-layouts  2.34 us (3%)
    pallas_call x1, Pallas kernels, local(): pl.pallas_call(kernel, out_shape=(jax.ShapeDtypeStruct((1,), F32), jax.Sh...  64.1 us
    unnamed x4, local copies, waits for them, and re-layouts  2.34 us

profile of v4, /device:TPU:1, one launch (start us, length us, event | category | flops | bytes accessed | tf_op | source)
XLA Modules:
  0.0 69.6 jit_solution(3046859925018110797)
XLA Ops:
  1.3 64.1 %shard_map.58 = (f32[1]{0:T(128)}, f32[128,384]{1,0:T(8,128)}, f32[128,384]{1,0:T(8,128)}) custom-call(f32[1]{0:T(128)S(6)} %copy.9.scale_ref, bf16[128,384]{1,0:T(8,128)(2,1)} %img_ref.1, bf16[128,384]{1,0:T(8,128)(2,1)} %txt_ref.1), custom_call_target="tpu_custom_call" | custom-call | flops 9663676416 | bytes 393216 | tf_op jit(solution)/shard_map/pallas_call | solution.py:401
  66.1 0.0 copy-start
  66.1 1.7 %copy.11 = f32[128,384]{1,0:T(8,128)} copy(f32[128,384]{1,0:T(8,128)} %get-tuple-element.7) | data formatting | bytes 393216
  67.8 0.0 copy-done
  67.8 0.7 copy.12
Async XLA Ops:
  66.1 1.7 %copy-start = (f32[128,384]{1,0:T(8,128)S(1)}, f32[128,384]{1,0:T(8,128)}, u32[]{:S(2)}) copy-start(f32[128,384]{1,0:T(8,128)} %get-tuple-element.8) | copy-start | bytes 589828

commit v5 on v4

--- a/solution.py
+++ b/solution.py
@@ -108,7 +108,7 @@
 
     prod = img_ref[...].astype(F32) * txt_ref[...].astype(F32)
     prod = prod[:, 0:128] + prod[:, 128:256] + prod[:, 256:384]
-    msg_r[16:24, :] = jnp.sum(prod.reshape(B // 8, 8, 128), 0)
+    msg_c[16:24, :] = jnp.sum(prod.reshape(B // 8, 8, 128), 0)
 
     def tile(k, j):
         row0 = k * R2
@@ -196,26 +196,17 @@
     for k in range(NZ):
         finish_rows(k)
 
-    for cc in range(COLS // 128):
-        lanes = slice(cc * 128, (cc + 1) * 128)
-        mt = cm_ref[:, :, lanes].reshape(NZ * 8, 128)
-        lt = cl_ref[:, :, lanes].reshape(NZ * 8, 128)
-        top = jnp.max(mt, 0, keepdims=True)
-        total = jnp.sum(lt * jnp.exp2(mt - top), 0, keepdims=True)
-        msg_c[cc : cc + 1, :] = top + jnp.log(total) * LOG2E
-
     def row_msg(d, r):
-        q = d * 2 + r
-        return rcopy(msg_r, got_r.at[q], mr_s, mr_r, dev(0, 0, d, r))
+        return rcopy(msg_r, got_r.at[d * 2 + r], mr_s, mr_r, dev(0, 0, d, r))
 
     def col_msg(i, j):
-        q = j * 4 + i
-        return rcopy(msg_c, got_c.at[q], mc_s, mc_r, dev_ab(i, j))
-
-    for d, r in row_peers:
-        row_msg(d, r).start()
-    for i, j in col_peers:
-        col_msg(i, j).start()
+        return rcopy(msg_c, got_c.at[j * 4 + i], mc_s, mc_r, dev_ab(i, j))
+
+    def a_msg(i, j):
+        return rcopy(out_a, got_a.at[j * 4 + i], la_s, la_r, dev_ab(i, j))
+
+    def b_msg(d, r):
+        return rcopy(out_b, got_b.at[d * 2 + r], lb_s, lb_r, dev(0, 0, d, r))
 
     def combine(parts):
         top = parts[0]
@@ -226,25 +217,47 @@
             total = total + jnp.exp2(p - top)
         return top + jnp.log(total) * LOG2E
 
+    for d in (4, 3, 5, 2, 6, 1, 7, 0):
+        for r in range(2):
+            if (d, r) != (0, 0):
+                row_msg(d, r).start()
+
+    for cc in range(COLS // 128):
+        lanes = slice(cc * 128, (cc + 1) * 128)
+        mt = cm_ref[:, :, lanes].reshape(NZ * 8, 128)
+        lt = cl_ref[:, :, lanes].reshape(NZ * 8, 128)
+        top = jnp.max(mt, 0, keepdims=True)
+        total = jnp.sum(lt * jnp.exp2(mt - top), 0, keepdims=True)
+        msg_c[cc : cc + 1, :] = top + jnp.log(total) * LOG2E
+
+    for i, j in reversed(col_peers):
+        col_msg(i, j).start()
+
     drain(got_r.at[pl.ds(1, 15)], mr_r)
     halves = ([], [])
-    diag = msg_r[16:24, :]
     for d in range(NZ):
         for r in range(2):
             ref = msg_r if (d, r) == (0, 0) else got_r.at[d * 2 + r]
-            if (d, r) != (0, 0):
-                diag = diag + ref[16:24, :]
             for rs in range(2):
                 v = ref[rs * 8 : rs * 8 + 8, :]
                 halves[rs ^ r].append(pltpu.roll(v, d, 0) if d else v)
     lr = [combine(h) for h in halves]
+    for k in range(NZ):
+        for r in range(2):
+            lrb_ref[k * R2 + r * B : k * R2 + (r + 1) * B, :] = (
+                jnp.broadcast_to(lr[r][k : k + 1, :], (B, 128)) + 1.0
+            ).T
 
     drain(got_c.at[pl.ds(1, 15)], mc_r)
     jj = lax.broadcasted_iota(jnp.int32, (NX * NY, 128), 0) % NY
     parts = []
+    diag = msg_c[16:24, :]
     for a in range(NX):
         for b in range(NY):
-            v = msg_c[...] if (a, b) == (0, 0) else got_c[a * NY + b]
+            ref = msg_c if (a, b) == (0, 0) else got_c.at[a * NY + b]
+            v = ref[0:16, :]
+            if (a, b) != (0, 0):
+                diag = diag + ref[16:24, :]
             s1, s2 = (4 * a + b) % 16, (4 * a + b + 12) % 16
             if b == 0:
                 v = pltpu.roll(v, s1, 0) if s1 else v
@@ -254,27 +267,14 @@
     lc = combine(parts)
     lc_ref[...] = lc + 1.0
 
-    out_a[...] = (lr[0] + lr[1]) * LN2 - (2.0 * factor) * diag
-    out_b[...] = (lc[0:8] + lc[8:16]) * LN2
-
-    def a_msg(i, j):
-        q = j * 4 + i
-        return rcopy(out_a, got_a.at[q], la_s, la_r, dev_ab(i, j))
-
-    def b_msg(d, r):
-        q = d * 2 + r
-        return rcopy(out_b, got_b.at[q], lb_s, lb_r, dev(0, 0, d, r))
-
-    for i, j in col_peers:
-        a_msg(i, j).start()
-    for d, r in row_peers:
-        b_msg(d, r).start()
-
-    for k in range(NZ):
-        for r in range(2):
-            lrb_ref[k * R2 + r * B : k * R2 + (r + 1) * B, :] = (
-                jnp.broadcast_to(lr[r][k : k + 1, :], (B, 128)) + 1.0
-            ).T
+    out_a[...] = (lr[0] + lr[1]) * LN2
+    out_b[...] = (lc[0:8] + lc[8:16]) * LN2 - (2.0 * factor) * diag
+
+    def send_shares():
+        for i, j in col_peers:
+            a_msg(i, j).start()
+        for d, r in row_peers:
+            b_msg(d, r).start()
 
     def sib_part(k):
         return rcopy(sib_out.at[k], sib_in.at[k], sb_s, sb_r.at[k], dev(0, 0, 0, 1))
@@ -331,23 +331,28 @@
         t_out[j] = third(j).astype(BF16)
         txt_part(j).start()
 
-    for j in (2, 1):
-        for k in range(NZ):
-            weigh(k, (j,))
-        send_quarter(j)
+    for k in range(NZ):
+        weigh(k, (2,))
+    send_quarter(2)
+    send_shares()
+    for k in range(NZ):
+        weigh(k, (1,))
+    send_quarter(1)
+    for k in range(NZ):
+        weigh(k, (3,))
+    send_quarter(3)
 
     ks = (4, 3, 5, 1, 7, 2, 6, 0)
-    weigh(ks[0], (0, 3))
+    weigh(ks[0], (0,))
     for n, k in enumerate(ks):
         if n < 7:
-            weigh(ks[n + 1], (0, 3))
+            weigh(ks[n + 1], (0,))
         part = jnp.dot(w_ref[k * R2 : (k + 1) * R2, :], txt_all[...], preferred_element_type=F32)
         keep_i[k] = part[0:B]
         sib_out[k] = part[B:R2]
         sib_part(k).start()
         if 1 <= n <= 5:
             pass_on(ks[n - 1])
-    send_quarter(3)
     pass_on(2)
     pass_on(6)
     keep_t[...] = third(0)
@@ -395,10 +400,16 @@
     drain(u_in.at[pl.ds(1, 3)], uo_s)
 
 
+def hand_over(loss_in, gi_in, gt_in, loss_ref, gi_ref, gt_ref):
+    loss_ref[0] = loss_in[0]
+    gi_ref[...] = gi_in[...]
+    gt_ref[...] = gt_in[...]
+
+
 def local(images, texts, logit_scale):
     dma = pltpu.SemaphoreType.DMA
     vm = pltpu.VMEM
-    return pl.pallas_call(
+    parts = pl.pallas_call(
         kernel,
         out_shape=(
             jax.ShapeDtypeStruct((1,), F32),
@@ -420,7 +431,7 @@
             vm((ROWS, COLS), F32), vm((ROWS, COLS), BF16),
             vm((4, ROWS, 128), F32), vm((4, ROWS, 128), F32), vm((NZ, 8, COLS), F32), vm((NZ, 8, COLS), F32),
             vm((ROWS, 128), F32), vm((16, 128), F32),
-            vm((24, 128), F32), vm((16, 128), F32), vm((16, 24, 128), F32), vm((16, 16, 128), F32),
+            vm((16, 128), F32), vm((24, 128), F32), vm((16, 16, 128), F32), vm((16, 24, 128), F32),
             vm((8, 128), F32), vm((8, 128), F32), vm((16, 8, 128), F32), vm((16, 8, 128), F32),
             vm((NZ, B, E), F32), vm((NZ, B, E), F32), vm((NZ, B, E), F32),
             vm((NZ, B, E), BF16), vm((NZ, B, E), BF16), vm((3, B, E), BF16),
@@ -436,6 +447,18 @@
             flops=6 * ROWS * COLS * E, bytes_accessed=8 * B * E, transcendentals=4 * ROWS * COLS
         ),
     )(logit_scale, images, texts)
+    return pl.pallas_call(
+        hand_over,
+        out_shape=(
+            jax.ShapeDtypeStruct((1,), F32),
+            jax.ShapeDtypeStruct((B, E), F32),
+            jax.ShapeDtypeStruct((B, E), F32),
+        ),
+        in_specs=[pl.BlockSpec(memory_space=pltpu.SMEM), pl.BlockSpec(memory_space=vm), pl.BlockSpec(memory_space=vm)],
+        out_specs=(
+            pl.BlockSpec(memory_space=pltpu.SMEM), pl.BlockSpec(memory_space=vm), pl.BlockSpec(memory_space=vm)
+        ),
+    )(*parts)
 
 
 def solution(mesh):

time: 69.7 us -> 65.4 us (0.938)
  local copies, waits for them, and re-layouts: 2.34 us -> 0 us
  between operations: 3.11 us -> 1.45 us
    pallas_call x1, Pallas kernels: 64.1 us -> 61.4 us  [local(): pl.pallas_call(kernel, out_shape=(jax.ShapeDtypeStruct((1,), F32), jax.Sh...]
    pallas_call x0 -> x1, Pallas kernels: none -> 2.41 us  [local(): pl.pallas_call(hand_over, out_shape=(jax.ShapeDtypeStruct((1,), F32), jax...]
    unnamed x4 -> x0, local copies, waits for them, and re-layouts: 2.34 us -> none
where the time goes in v5:
time: 65.4 us; the launch traced here: 65.3 us
  Pallas kernels  63.8 us (98%)
  between operations  1.45 us (2%)
    pallas_call x1, Pallas kernels, local(): pl.pallas_call(kernel, out_shape=(jax.ShapeDtypeStruct((1,), F32), jax.Sh...  61.4 us
    pallas_call x1, Pallas kernels, local(): pl.pallas_call(hand_over, out_shape=(jax.ShapeDtypeStruct((1,), F32), jax...  2.41 us

profile of v5, /device:TPU:1, one launch (start us, length us, event | category | flops | bytes accessed | tf_op | source)
XLA Modules:
  0.0 65.3 jit_solution(7331976738718275707)
XLA Ops:
  1.3 61.4 %shard_map.58 = (f32[1]{0:T(128)}, f32[128,384]{1,0:T(8,128)}, f32[128,384]{1,0:T(8,128)}) custom-call(f32[1]{0:T(128)S(6)} %copy.6.scale_ref, bf16[128,384]{1,0:T(8,128)(2,1)} %img_ref.1, bf16[128,384]{1,0:T(8,128)(2,1)} %txt_ref.1), custom_call_target="tpu_custom_call" | custom-call | flops 9663676416 | bytes 393216 | tf_op jit(solution)/shard_map/pallas_call | solution.py:412
  62.7 2.4 %shard_map.59 = (f32[1]{0:T(128)}, f32[128,384]{1,0:T(8,128)}, f32[128,384]{1,0:T(8,128)}) custom-call(f32[1]{0:T(128)} %get-tuple-element.6.loss_in, f32[128,384]{1,0:T(8,128)} %get-tuple-element.7.gi_in, f32[128,384]{1,0:T(8,128)} %get-tuple-element.8.gt_in), custom_call_target="tpu_custom_call" | custom-call | tf_op jit(solution)/shard_map/pallas_call | solution.py:450

commit v6 on v5

--- a/solution.py
+++ b/solution.py
@@ -102,7 +102,7 @@
         txt_first(i).start()
     for k in (2, 6, 1, 7):
         img_copy(k).start()
-    for j in (1, 3, 2):
+    for j in (1, 3):
         txt_second(0, j).start()
     sib_copy(0).start()
 
@@ -151,8 +151,10 @@
 
     for i in (1, 3, 2):
         txt_first(i).wait_recv()
-        for j in (1, 3, 2):
+        for j in (1, 3):
             txt_second(i, j).start()
+    for i in range(4):
+        txt_second(i, 2).start()
     sib_copy(0).wait_recv()
     img_copy(2).wait_recv()
     img_forward(3).start()
@@ -190,11 +192,12 @@
     turn(5)
     txt_quarter(2)
     tiles((0, 2, 6, 1, 7, 3, 5), (2,))
+    for k in (0, 2, 6, 1, 7, 3, 5):
+        finish_rows(k)
     sib_copy(4).wait_recv()
     tiles((4,), (0, 1, 3, 2))
+    finish_rows(4)
     turn(4)
-    for k in range(NZ):
-        finish_rows(k)
 
     def row_msg(d, r):
         return rcopy(msg_r, got_r.at[d * 2 + r], mr_s, mr_r, dev(0, 0, d, r))
@@ -342,17 +345,26 @@
         weigh(k, (3,))
     send_quarter(3)
 
-    ks = (4, 3, 5, 1, 7, 2, 6, 0)
-    weigh(ks[0], (0,))
-    for n, k in enumerate(ks):
-        if n < 7:
-            weigh(ks[n + 1], (0,))
-        part = jnp.dot(w_ref[k * R2 : (k + 1) * R2, :], txt_all[...], preferred_element_type=F32)
-        keep_i[k] = part[0:B]
-        sib_out[k] = part[B:R2]
-        sib_part(k).start()
-        if 1 <= n <= 5:
-            pass_on(ks[n - 1])
+    pairs = (4, 2, 6, 0)
+    weigh(4, (0,))
+    weigh(5, (0,))
+    for n, k in enumerate(pairs):
+        if n < 3:
+            weigh(pairs[n + 1], (0,))
+            weigh(pairs[n + 1] + 1, (0,))
+        part = jnp.dot(w_ref[k * R2 : (k + 2) * R2, :], txt_all[...], preferred_element_type=F32)
+        for h in (1, 0) if k == 2 else (0, 1):
+            keep_i[k + h] = part[h * R2 : h * R2 + B]
+            sib_out[k + h] = part[h * R2 + B : (h + 1) * R2]
+            sib_part(k + h).start()
+        if n == 1:
+            pass_on(4)
+            pass_on(5)
+        if n == 2:
+            pass_on(3)
+        if n == 3:
+            pass_on(7)
+    pass_on(1)
     pass_on(2)
     pass_on(6)
     keep_t[...] = third(0)

time: 65.4 us -> 65.1 us (level)
  no operation moved by 1% of the time
where the time goes in v6:
time: 65.1 us; the launch traced here: 64.9 us
  Pallas kernels  63.5 us (98%)
  between operations  1.45 us (2%)
    pallas_call x1, Pallas kernels, local(): pl.pallas_call(kernel, out_shape=(jax.ShapeDtypeStruct((1,), F32), jax.Sh...  61.1 us
    pallas_call x1, Pallas kernels, local(): pl.pallas_call(hand_over, out_shape=(jax.ShapeDtypeStruct((1,), F32), jax...  2.41 us

profile of v6, /device:TPU:1, one launch (start us, length us, event | category | flops | bytes accessed | tf_op | source)
XLA Modules:
  0.0 64.9 jit_solution(8147172437206850259)
XLA Ops:
  1.3 61.1 %shard_map.58 = (f32[1]{0:T(128)}, f32[128,384]{1,0:T(8,128)}, f32[128,384]{1,0:T(8,128)}) custom-call(f32[1]{0:T(128)S(6)} %copy.6.scale_ref, bf16[128,384]{1,0:T(8,128)(2,1)} %img_ref.1, bf16[128,384]{1,0:T(8,128)(2,1)} %txt_ref.1), custom_call_target="tpu_custom_call" | custom-call | flops 9663676416 | bytes 393216 | tf_op jit(solution)/shard_map/pallas_call | solution.py:424
  62.4 2.4 %shard_map.59 = (f32[1]{0:T(128)}, f32[128,384]{1,0:T(8,128)}, f32[128,384]{1,0:T(8,128)}) custom-call(f32[1]{0:T(128)} %get-tuple-element.6.loss_in, f32[128,384]{1,0:T(8,128)} %get-tuple-element.7.gi_in, f32[128,384]{1,0:T(8,128)} %get-tuple-element.8.gt_in), custom_call_target="tpu_custom_call" | custom-call | tf_op jit(solution)/shard_map/pallas_call | solution.py:462

commit v7 on v6

--- a/solution.py
+++ b/solution.py
@@ -61,11 +61,11 @@
     barrier = pltpu.get_barrier_semaphore()
     row_peers = [(d, r) for d in range(NZ) for r in range(2) if (d, r) != (0, 0)]
     col_peers = [(i, j) for i in range(NX) for j in range(NY) if (i, j) != (0, 0)]
-    for d, r in row_peers:
-        pl.semaphore_signal(barrier, inc=1, device_id=dev(0, 0, d, r), device_id_type=MESH)
-    for i, j in col_peers:
-        pl.semaphore_signal(barrier, inc=1, device_id=dev_ab(i, j), device_id_type=MESH)
-    pl.semaphore_wait(barrier, len(row_peers) + len(col_peers))
+    near = [dev_ab(i, 0) for i in (1, 3, 2)] + [dev_ab(0, j) for j in (1, 3, 2)]
+    near += [dev(0, 0, d, 0) for d in (1, 7, 2, 6)] + [dev(0, 0, 0, 1)]
+    for to in near:
+        pl.semaphore_signal(barrier, inc=1, device_id=to, device_id_type=MESH)
+    pl.semaphore_wait(barrier, len(near))
 
     def img_rows(k, h=None):
         return img_all.at[pl.ds(k * R2, B)] if h is None else img_all.at[pl.ds(k * R2 + h * 64, 64)]

time: 65.1 us -> 63.9 us (0.982)
  Pallas kernels: 63.5 us -> 62.3 us
    pallas_call x1, Pallas kernels: 61.1 us -> 59.9 us  [local(): pl.pallas_call(kernel, out_shape=(jax.ShapeDtypeStruct((1,), F32), jax.Sh...]
where the time goes in v7:
time: 63.9 us; the launch traced here: 63.8 us
  Pallas kernels  62.3 us (97%)
  between operations  1.45 us (2%)
    pallas_call x1, Pallas kernels, local(): pl.pallas_call(kernel, out_shape=(jax.ShapeDtypeStruct((1,), F32), jax.Sh...  59.9 us
    pallas_call x1, Pallas kernels, local(): pl.pallas_call(hand_over, out_shape=(jax.ShapeDtypeStruct((1,), F32), jax...  2.41 us

profile of v7, /device:TPU:1, one launch (start us, length us, event | category | flops | bytes accessed | tf_op | source)
XLA Modules:
  0.0 63.8 jit_solution(3750319123918088931)
XLA Ops:
  1.3 59.9 %shard_map.58 = (f32[1]{0:T(128)}, f32[128,384]{1,0:T(8,128)}, f32[128,384]{1,0:T(8,128)}) custom-call(f32[1]{0:T(128)S(6)} %copy.6.scale_ref, bf16[128,384]{1,0:T(8,128)(2,1)} %img_ref.1, bf16[128,384]{1,0:T(8,128)(2,1)} %txt_ref.1), custom_call_target="tpu_custom_call" | custom-call | flops 9663676416 | bytes 393216 | tf_op jit(solution)/shard_map/pallas_call | solution.py:424
  61.2 2.4 %shard_map.59 = (f32[1]{0:T(128)}, f32[128,384]{1,0:T(8,128)}, f32[128,384]{1,0:T(8,128)}) custom-call(f32[1]{0:T(128)} %get-tuple-element.6.loss_in, f32[128,384]{1,0:T(8,128)} %get-tuple-element.7.gi_in, f32[128,384]{1,0:T(8,128)} %get-tuple-element.8.gt_in), custom_call_target="tpu_custom_call" | custom-call | tf_op jit(solution)/shard_map/pallas_call | solution.py:462
